TPU v7x, 32 devices: a whole 2x2x4 slice. The times are simulated.
32 devices in a mesh: groups: 2 (over x), rep: 16 (over z, y, core).
Axes of the slice: x: 2, y: 2, z: 4, core: 2. Of those that a mesh axis runs over, the one named last changes fastest.
Arguments:
- normed_input_rows: bfloat16 [256, 8192], P(('groups', 'rep')), parts along dimension 0, may hold values from -6 to 6
- counts: int32 [32, 8], P('groups'), parts along dimension 0, may hold values from 0 to 8, as said below
- gate_weight_matrix: bfloat16 [8192, 28672], P(None, 'rep'), may hold values from -0.0625 to 0.0625
- up_weight_matrix: bfloat16 [8192, 28672], P(None, 'rep'), may hold values from -0.0625 to 0.0625
- adapter_down_weight: bfloat16 [16, 8192, 128], P('groups', 'rep'), parts along dimension 0, may hold values from -0.0625 to 0.0625
- adapter_gate_weight: bfloat16 [16, 64, 28672], P('groups', None, 'rep'), parts along dimension 0, may hold values from -0.75 to 0.75
- adapter_up_weight: bfloat16 [16, 64, 28672], P('groups', None, 'rep'), parts along dimension 0, may hold values from -0.75 to 0.75
Outputs:
- hidden: bfloat16 [256, 28672], P('groups', 'rep'), parts along dimension 0
There are 2 independent parts, one for each index of `groups`. A program takes and returns all parts, laid end to end along the dimension named above; an argument that names none is the same for every part. Nothing has to cross between parts.
Inputs may be any that keep to these rules, and one draw needn't show every extreme that they name: Each row of counts sums to 8; a replica's rows stand in order of version.
All inputs are finite; a program needn't handle non-finite values.
Results may differ from a plain program's by a relative error of at most 0.0056.
Values may be sent and summed in bfloat16 or wider, within the bound.
No kernel may reach another device: no remote copies, remote signals or barrier semaphores. Data moves between devices by JAX's collectives and lax.ppermute only.
A program may use at most 192 MiB of HBM per device.

v0:
```python
import jax
import jax.numpy as jnp
from jax import lax
from jax.sharding import PartitionSpec as P

ADAPTER_RANK = 64
POLICY_VERSIONS = 8
ROWS_DEV = 8


adapter_scale = 2.0


def row_versions(counts):
    running = jnp.cumsum(counts, axis=1)
    place = jnp.arange(ROWS_DEV, dtype=jnp.int32)
    version = jnp.sum((running[:, None, :] <= place[None, :, None]).astype(jnp.int32), axis=2)
    return version.reshape(-1)


def spread_rank(onehot, factors):
    total_rows = factors.shape[0]
    widened = onehot[:, :, None] * factors.astype(jnp.float32)[:, None, :]
    return widened.reshape(total_rows, POLICY_VERSIONS * ADAPTER_RANK).astype(jnp.bfloat16)


def local(
    normed_input_rows,
    counts,
    gate_weight_matrix,
    up_weight_matrix,
    adapter_down_weight,
    adapter_gate_weight,
    adapter_up_weight,
):
    version = row_versions(counts)
    onehot_all = (version[:, None] == jnp.arange(POLICY_VERSIONS, dtype=jnp.int32)[None, :]).astype(
        jnp.float32
    )
    hidden_local = gate_weight_matrix.shape[1]
    feat_count = adapter_down_weight.shape[1]
    feat_start = lax.axis_index("rep") * feat_count
    piece = lax.all_gather(normed_input_rows, "rep", axis=0, tiled=True)
    feat_slice = lax.dynamic_slice_in_dim(piece, feat_start, feat_count, 1)
    every_version_output = jnp.einsum(
        "tj,bjo->tbo", feat_slice, adapter_down_weight, preferred_element_type=jnp.float32
    )
    partial_sum = jnp.sum(every_version_output * onehot_all[:, :, None], axis=1)
    base_gate = jnp.dot(piece, gate_weight_matrix, preferred_element_type=jnp.float32)
    base_up = jnp.dot(piece, up_weight_matrix, preferred_element_type=jnp.float32)
    combined_down = jnp.concatenate([base_gate, base_up, partial_sum], axis=1)
    shrink = lax.psum(combined_down[:, 2 * hidden_local :], "rep").astype(jnp.bfloat16)
    expanded_gate = spread_rank(onehot_all, shrink[:, :ADAPTER_RANK])
    expanded_up = spread_rank(onehot_all, shrink[:, ADAPTER_RANK:])
    gate_output = combined_down[:, :hidden_local] + adapter_scale * jnp.dot(
        expanded_gate,
        adapter_gate_weight.reshape(POLICY_VERSIONS * ADAPTER_RANK, hidden_local),
        preferred_element_type=jnp.float32,
    )
    up_output = combined_down[:, hidden_local : 2 * hidden_local] + adapter_scale * jnp.dot(
        expanded_up,
        adapter_up_weight.reshape(POLICY_VERSIONS * ADAPTER_RANK, hidden_local),
        preferred_element_type=jnp.float32,
    )
    return (jax.nn.silu(gate_output) * up_output).astype(jnp.bfloat16)


def solution(mesh):
    placed = (
        P(("groups", "rep"), None),
        P("groups", None),
        P(None, "rep"),
        P(None, "rep"),
        P("groups", "rep", None),
        P("groups", None, "rep"),
        P("groups", None, "rep"),
    )
    return jax.shard_map(
        local, mesh=mesh, in_specs=placed, out_specs=P("groups", "rep"), check_vma=False
    )
```

profile of v0, /device:TPU:0, one launch (start us, length us, event | category | flops | bytes accessed | tf_op | source)
XLA Modules:
  0.0 149.2 jit_solution(14592284784511987763)
XLA Ops:
  6.5 0.0 copy-start
  6.5 0.0 all-gather.2.cloned.1.call-start
  6.5 0.7 all-gather.2.cloned.1.call-update
  7.3 0.7 reduce_window_sum.11
  8.0 0.1 copy.16
  8.1 0.1 eq.19
  8.2 45.5 %all-gather.2.cloned.1.call-done = bf16[128,8192]{1,0:T(8,128)(2,1)} async-done(((bf16[8,8192]{1,0:T(8,128)(2,1)}), bf16[128,8192]{1,0:T(8,128)(2,1)}) %all-gather.2.cloned.1.call-update) | async-done | bytes 2097168 | tf_op jit(solution)/shard_map/all_gather | solution.py:43
  53.7 1.6 %fusion.6 = f32[128,128]{1,0:T(8,128)S(1)} fusion(bf16[8,512,128]{2,1,0:T(8,128)(2,1)} %param.11, f32[128,8]{0,1:T(8,128)S(1)} %fusion.13, bf16[128,8192]{1,0:T(8,128)(2,1)} %all-gather.2.cloned.1.call-done, s32[]{:T(128)S(6)} %select_n.3), kind=kOutput, calls=%fused_computation.9 | convolution fusion | flops 134463488 | bytes 1249284 | tf_op jit(solution)/shard_map/tj,bjo->tbo/dot_general | solution.py:45
  55.3 0.1 copy.17
  55.4 59.6 %psum.7 = bf16[128,128]{0,1:T(8,128)(2,1)S(1)} all-reduce(f32[128,128]{0,1:T(8,128)S(1)} %copy.17), channel_id=1, replica_groups=mesh['groups'=2,'rep'=16] {'rep'}, use_global_device_ids=true, to_apply=%region_3.4 | all-reduce | flops 16384 | bytes 98304 | tf_op jit(solution)/shard_map/psum | solution.py:52
  114.9 12.3 %fusion.15 = f32[128,1792]{1,0:T(8,128)S(1)} fusion(bf16[128,8192]{1,0:T(8,128)(2,1)} %all-gather.2.cloned.1.call-done, bf16[8192,1792]{1,0:T(8,128)(2,1)} %param.9), kind=kOutput, calls=%fused_computation.25 | convolution fusion | flops 3758096384 | bytes 32374784 | tf_op jit(solution)/shard_map/dot_general | solution.py:49
  127.3 0.0 copy-start.2
  127.3 0.0 copy-done
  127.3 0.4 fusion.4
  127.7 1.1 copy-done.2
  128.9 0.0 copy-start.3
  128.9 11.9 %fusion.16 = f32[128,1792]{1,0:T(8,128)S(1)} fusion(bf16[128,8192]{1,0:T(8,128)(2,1)S(1)} %copy-done.2, bf16[8192,1792]{1,0:T(8,128)(2,1)} %param.10), kind=kOutput, calls=%fused_computation.26 | convolution fusion | flops 3758096384 | bytes 32374784 | tf_op jit(solution)/shard_map/dot_general | solution.py:50
  140.8 0.0 copy-start.1
  140.8 0.0 copy-done.3
  140.8 1.3 fusion.5
  142.2 0.1 copy-done.1
  (3 shorter events, 0.0 us)
Async XLA Ops:
  6.5 120.8 %copy-start = (bf16[8,64,1792]{2,1,0:T(8,128)(2,1)S(1)}, bf16[8,64,1792]{2,1,0:T(8,128)(2,1)}, u32[]{:S(2)}) copy-start(bf16[8,64,1792]{2,1,0:T(8,128)(2,1)} %param.12) | copy-start | bytes 5505028
  6.5 47.1 %all-gather.2.cloned.1.call-start = ((), (), s32[]{:S(2)}) async-start(), calls=%async_computation | async-start | bytes 2228224 | tf_op jit(solution)/shard_map/all_gather | solution.py:43
  127.3 1.6 %copy-start.2 = (bf16[128,8192]{1,0:T(8,128)(2,1)S(1)}, bf16[128,8192]{1,0:T(8,128)(2,1)}, u32[]{:S(2)}) copy-start(bf16[128,8192]{1,0:T(8,128)(2,1)} %all-gather.2.cloned.1.call-done) | copy-start | bytes 6291460
  128.9 12.0 %copy-start.3 = (bf16[8,64,1792]{2,1,0:T(8,128)(2,1)S(1)}, bf16[8,64,1792]{2,1,0:T(8,128)(2,1)}, u32[]{:S(2)}) copy-start(bf16[8,64,1792]{2,1,0:T(8,128)(2,1)} %param.13) | copy-start | bytes 5505028
  140.8 1.5 %copy-start.1 = (bf16[8,64,1792]{2,1,0:T(8,128)(2,1)S(1)}, bf16[8,64,1792]{2,1,0:T(8,128)(2,1)}, u32[]{:S(2)}) copy-start(bf16[8,64,1792]{2,1,0:T(8,128)(2,1)} %param.12) | copy-start | bytes 5505028
Sparse Core Ops, SparseCore 0:
  9.5 44.0 all-gather.1
where the time goes:
time: 149 us
  blocking collectives  59.6 us (40%)
  waiting for transfers between devices  46.2 us (31%)
  matrix products  27.7 us (19%)
  between operations  13.5 us (9%)
  local copies, waits for them, and re-layouts  1.52 us (1%)
    psum x1, blocking collectives, local(): lax.psum(combined_down[:, 2 * hidden_local:], 'rep').astype(jnp.bfloat16)  59.6 us
    all_gather x1, waiting for transfers between devices, local(): piece = lax.all_gather(normed_input_rows, 'rep', axis=0, tiled=True)  45.5 us
    dot_general x1, matrix products, local(): jnp.dot(piece, gate_weight_matrix, preferred_element_type=jnp.float32)  12.3 us
    dot_general x1, matrix products, local(): jnp.dot(piece, up_weight_matrix, preferred_element_type=jnp.float32)  11.9 us
  transfers between devices with their start and end apart: 1, of which 1 were waited for; matrix products, arithmetic and copies ran while one was open for 1% of the time, Pallas kernels for 0%

commit v1 on v0

--- a/solution.py
+++ b/solution.py
@@ -1,14 +1,270 @@
+import functools
+
 import jax
 import jax.numpy as jnp
 from jax import lax
+from jax.experimental import pallas as pl
+from jax.experimental.pallas import tpu as pltpu
 from jax.sharding import PartitionSpec as P
 
 ADAPTER_RANK = 64
 POLICY_VERSIONS = 8
 ROWS_DEV = 8
-
-
 adapter_scale = 2.0
+
+F32, BF16 = jnp.float32, jnp.bfloat16
+MiB = 2**20
+VM = pl.BlockSpec(memory_space=pltpu.VMEM)
+HB = pl.BlockSpec(memory_space=pltpu.HBM)
+LANE_BITS = ((4, 2, 1), (1, 4, 2))
+
+
+def dot(a, b):
+    return jnp.dot(a, b, preferred_element_type=F32)
+
+
+def place():
+    me = lax.axis_index("rep")
+    return me // 2, lax.rem(me, 2)
+
+
+def call(body, outs, ins, specs=None, scratch=(), vmem=2, bytes_=0, flops=0, alias=None, out_specs=None):
+    return pl.pallas_call(
+        body,
+        out_shape=outs,
+        in_specs=[VM] * len(ins) if specs is None else specs,
+        out_specs=jax.tree.map(lambda _: VM, outs),
+        scratch_shapes=list(scratch),
+        input_output_aliases=alias or {},
+        compiler_params=pltpu.CompilerParams(vmem_limit_bytes=int(vmem * MiB)),
+        cost_estimate=pl.CostEstimate(flops=int(flops), bytes_accessed=int(bytes_), transcendentals=0),
+    )(*ins)
+
+
+def like(rows, cols, dtype=BF16):
+    return jax.ShapeDtypeStruct((rows, cols), dtype)
+
+
+def prep(x_ref, c_ref, m_ref, s_ref, o_ref):
+    o_ref[...] = c_ref[...]
+    _, core = place()
+    for q in range(8):
+        for lane, to_ref in ((core, m_ref), (1 - core, s_ref)):
+            cols = pl.ds(pl.multiple_of((2 * q + lane) * 512, 512), 512)
+            to_ref[:, q * 512 : q * 512 + 512] = x_ref[:, cols]
+
+
+def pair(m_ref, r_ref, o_ref):
+    _, core = place()
+    mine, other = m_ref[...], r_ref[...]
+    first = jnp.where(core == 0, mine, other)
+    second = jnp.where(core == 0, other, mine)
+    o_ref[...] = jnp.concatenate([first, second], axis=0)
+
+
+def double(step, m_ref, r_ref, o_ref):
+    chip, core = place()
+    rows = m_ref.shape[0]
+    bit = jnp.where(core == 0, lax.rem(chip // LANE_BITS[0][step], 2), lax.rem(chip // LANE_BITS[1][step], 2))
+    o_ref[pl.ds(pl.multiple_of(bit * rows, rows), rows), :] = m_ref[...]
+    o_ref[pl.ds(pl.multiple_of((1 - bit) * rows, rows), rows), :] = r_ref[...]
+
+
+def settle(m_ref, r_ref, o_ref):
+    chip, core = place()
+    for lane, (b0, b1, b2) in enumerate(LANE_BITS):
+
+        @pl.when(core == lane)
+        def _(b0=b0, b1=b1, b2=b2):
+            last = lax.rem(chip // b2, 2)
+            for i in range(4):
+                base = b0 * (i & 1) + b1 * (i >> 1)
+                for ref, bit in ((m_ref, last), (r_ref, 1 - last)):
+                    to = pl.multiple_of((base + b2 * bit) * 16, 16)
+                    o_ref[pl.ds(to, 16), :] = ref[i * 16 : i * 16 + 16, :]
+
+
+def versions(c_ref, o_ref):
+    rows, reps = o_ref.shape[0], c_ref.shape[1]
+    row = lax.broadcasted_iota(jnp.int32, (rows, reps), 0)
+    holds = (row // ROWS_DEV == lax.broadcasted_iota(jnp.int32, (rows, reps), 1)).astype(F32)
+    counts = lax.dot_general(holds, c_ref[...].astype(F32), (((1,), (1,)), ((), ())), preferred_element_type=F32)
+    spot = lax.rem(lax.broadcasted_iota(jnp.int32, (rows, 1), 0), ROWS_DEV).astype(F32)
+    running = jnp.zeros_like(spot)
+    version = jnp.zeros((rows, 1), jnp.int32)
+    for v in range(POLICY_VERSIONS):
+        running = running + counts[:, v : v + 1]
+        version = version + (running <= spot).astype(jnp.int32)
+    o_ref[...] = jnp.broadcast_to(version, o_ref.shape)
+
+
+def partial(x_ref, d_ref, v_ref, o_ref):
+    chip, _ = place()
+    x = x_ref[:, pl.ds(pl.multiple_of(chip * 512, 512), 512)]
+    version = v_ref[...]
+    total = jnp.zeros(o_ref.shape, F32)
+    for v in range(POLICY_VERSIONS):
+        total = total + jnp.where(version == v, dot(x, d_ref[v]), 0.0)
+    o_ref[...] = total
+
+
+def add(a_ref, b_ref, o_ref):
+    o_ref[...] = a_ref[...] + b_ref[...]
+
+
+HALF = 2
+
+
+def copies_of(units, hbm_refs, to_refs, sem):
+    _, core = place()
+    copies = []
+    for i, ((matrix, other, half), to_ref) in enumerate(zip(units, to_refs)):
+        lane = 1 - core if other else core
+        for k in range(HALF):
+            row = pl.multiple_of((2 * (half * HALF + k) + lane) * 512, 512)
+            copies.append(
+                pltpu.make_async_copy(
+                    hbm_refs[matrix].at[pl.ds(row, 512), :], to_ref.at[pl.ds(k * 512, 512), :], sem.at[i * HALF + k]
+                )
+            )
+    return copies
+
+
+def work(todo, xs, have, units, hbm, totals):
+    rows, cols = 128, hbm[0].shape[1]
+    done = sorted({m for m, _, _ in todo})
+    used = sorted({o for _, o, _ in todo})
+    old = [m for m in done if totals[m] is not None]
+    nt, nu = len(todo), len(units)
+
+    def body(*refs):
+        refs = list(refs)
+
+        def take(n):
+            got, refs[:] = refs[:n], refs[n:]
+            return got
+
+        x_refs = dict(zip(used, take(len(used))))
+        w_refs = take(nt)
+        hbm_refs = take(2)
+        old_refs = dict(zip(old, take(len(old))))
+        new_refs = dict(zip(done, take(len(done))))
+        to_refs = take(nu)
+        copies = copies_of(units, hbm_refs, to_refs, refs[0]) if nu else []
+        for c in copies:
+            c.start()
+        _, core = place()
+
+        @pl.when(core >= 0)
+        def _():
+            for m in done:
+                for n in range(0, cols, 256):
+                    total = old_refs[m][:, n : n + 256] if m in old_refs else None
+                    for (m2, other, half), w_ref in zip(todo, w_refs):
+                        if m2 == m:
+                            x = x_refs[other][:, half * HALF * 512 : (half + 1) * HALF * 512]
+                            term = dot(x, w_ref[:, n : n + 256])
+                            total = term if total is None else total + term
+                    new_refs[m][:, n : n + 256] = total
+
+        for c in copies:
+            c.wait()
+
+    ins = [xs[o] for o in used] + [have[t] for t in todo]
+    specs = [VM] * len(ins) + [HB] * 2 + [VM] * len(old)
+    ins += hbm
+    alias = {len(ins) + i: done.index(m) for i, m in enumerate(old)}
+    ins += [totals[m] for m in old]
+    outs = [like(rows, cols, F32) for _ in done] + [like(HALF * 512, cols) for _ in units]
+    got = call(
+        body, outs, ins, specs, [pltpu.SemaphoreType.DMA((nu * HALF,))] if nu else [], vmem=4, alias=alias,
+        bytes_=HALF * 512 * cols * 2 * max(nt, nu), flops=2 * rows * HALF * 512 * cols * nt,
+    )
+    for m, t in zip(done, got):
+        totals[m] = t
+    for unit, w in zip(units, got[len(done) :]):
+        have[unit] = pltpu.with_memory_space_constraint(w, pltpu.VMEM)
+    return got
+
+
+def finish(tg_ref, tu_ref, s_ref, r_ref, v_ref, ag_ref, au_ref, o_ref):
+    shrink = s_ref[...] + r_ref[...]
+    turned = pltpu.roll(shrink, ADAPTER_RANK, 1)
+    low = lax.broadcasted_iota(jnp.int32, shrink.shape, 1) < ADAPTER_RANK
+    version = v_ref[...]
+    half = (lax.broadcasted_iota(jnp.int32, shrink.shape, 1) >= ADAPTER_RANK).astype(jnp.int32)
+    wide = []
+    for twice in (jnp.where(low, shrink, turned), jnp.where(low, turned, shrink)):
+        parts = [jnp.where(version == 2 * k + half, twice, 0.0).astype(BF16) for k in range(POLICY_VERSIONS // 2)]
+        wide.append(jnp.concatenate(parts, axis=1))
+    for n in range(0, o_ref.shape[1], 256):
+        gate = tg_ref[:, n : n + 256] + adapter_scale * dot(wide[0], ag_ref[:, n : n + 256])
+        up = tu_ref[:, n : n + 256] + adapter_scale * dot(wide[1], au_ref[:, n : n + 256])
+        o_ref[:, n : n + 256] = (gate / (1.0 + jnp.exp(-gate)) * up).astype(BF16)
+
+
+def cores(n):
+    return [(i, i ^ 1) for i in range(n)]
+
+
+def lanes(step):
+    return [(2 * c + k, 2 * (c ^ LANE_BITS[k][step]) + k) for c in range(8) for k in range(2)]
+
+
+def chips(bit):
+    return [(i, i ^ (2 * bit)) for i in range(16)]
+
+
+def permute(x, pairs):
+    return lax.ppermute(x, "rep", pairs)
+
+
+PLAN = (1, 4, 4)
+AFTER = (3, 4, 0, 0)
+
+
+def split(items, sizes):
+    return [items[sum(sizes[:i]) : sum(sizes[: i + 1])] for i in range(len(sizes))]
+
+
+def hold(*values):
+    return lax.optimization_barrier(values)
+
+
+def tuned(x, counts, g, u, down, ag, au):
+    cols = g.shape[1]
+    hbm = [pltpu.with_memory_space_constraint(w, pltpu.HBM) for w in (g, u)]
+    rows = counts.shape[0] * ROWS_DEV
+    order = [(m, o, h) for o in range(2) for h in range(8 // HALF) for m in range(2)]
+    plan = split(order, PLAN)
+    have, totals = {}, [None, None]
+    mine, send, counts = call(prep, [like(8, 4096)] * 2 + [like(POLICY_VERSIONS, rows // ROWS_DEV, jnp.int32)], (x, counts.T))
+    a = call(pair, like(16, 4096), (mine, permute(send, cores(16))))
+    version = call(versions, like(rows, 128, jnp.int32), (counts,))
+    for step in range(3):
+        r = permute(a, lanes(step))
+        work([], [], have, plan[step], hbm, totals)
+        last = plan[step][-1]
+        if step == 0:
+            r, version, have[last] = hold(r, version, have[last])
+        else:
+            r, have[last] = hold(r, have[last])
+        body = functools.partial(double, step) if step < 2 else settle
+        a = call(body, like(a.shape[0] * 2, 4096), (a, r))
+    other = permute(a, cores(16))
+    xs = [a, other]
+    part = call(partial, like(rows, 128, F32), (a, down, version))
+    got = permute(part, cores(16))
+    after = split(order[sum(PLAN) :], AFTER)
+    for j in range(4):
+        todo = order[4 * j : 4 * j + 4]
+        work(todo, xs, have, after[j], hbm, totals)
+        if j < 3:
+            got, totals[0] = hold(got, totals[0])
+            part = call(add, like(rows, 128, F32), (part, got))
+            got = permute(part, chips((4, 2, 1)[j]))
+    wide = POLICY_VERSIONS * ADAPTER_RANK
+    return call(finish, like(rows, cols), (*totals, part, got, version, ag.reshape(wide, cols), au.reshape(wide, cols)), vmem=6)
 
 
 def row_versions(counts):
@@ -24,7 +280,7 @@
     return widened.reshape(total_rows, POLICY_VERSIONS * ADAPTER_RANK).astype(jnp.bfloat16)
 
 
-def local(
+def general(
     normed_input_rows,
     counts,
     gate_weight_matrix,
@@ -75,6 +331,5 @@
         P("groups", None, "rep"),
         P("groups", None, "rep"),
     )
-    return jax.shard_map(
-        local, mesh=mesh, in_specs=placed, out_specs=P("groups", "rep"), check_vma=False
-    )
+    local = tuned if mesh.shape["rep"] == 16 else general
+    return jax.shard_map(local, mesh=mesh, in_specs=placed, out_specs=P("groups", "rep"), check_vma=False)

time: 149 us -> 53.2 us (0.36)
  blocking collectives: 59.6 us -> 0 us
  waiting for transfers between devices: 46.2 us -> 4.38 us
  Pallas kernels: 0 us -> 29.4 us
  matrix products: 27.7 us -> 0 us
  starting transfers between devices: 0.01 us -> 17.5 us
  between operations: 13.5 us -> 0.18 us
    psum x1 -> x0, blocking collectives: 59.6 us -> none  [local(): lax.psum(combined_down[:, 2 * hidden_local:], 'rep').astype(jnp.bfloat16)]
    all_gather x1 -> x0, waiting for transfers between devices: 45.5 us -> none  [local(): piece = lax.all_gather(normed_input_rows, 'rep', axis=0, tiled=True)]
    pallas_call x0 -> x18, Pallas kernels: none -> 29.4 us  [call(): pl.pallas_call(body, out_shape=outs, in_specs=[VM] * len(ins) if specs is...]
    dot_general x5 -> x0, matrix products: 27.7 us -> none  [the longest x1 12.3 us: local(): jnp.dot(piece, gate_weight_matrix, preferred_element_type=jnp.float32)]
    ppermute x0 -> x9, starting transfers between devices: none -> 17.5 us  [permute(): return lax.ppermute(x, 'rep', pairs)]
    ppermute x0 -> x9, waiting for transfers between devices: none -> 4.38 us  [permute(): return lax.ppermute(x, 'rep', pairs)]
  transfers between devices with their start and end apart: 1 -> 9, of which waited for: 1 -> 5; matrix products, arithmetic and copies ran while one was open for 1% -> 0% of each run, Pallas kernels for 0% -> 52%
where the time goes in v1:
time: 53.2 us; the launch traced here: 53 us
  Pallas kernels  29.4 us (55%)
  starting transfers between devices  17.5 us (33%)
  waiting for transfers between devices  4.38 us (8%)
  local copies, waits for them, and re-layouts  1.6 us (3%)
    pallas_call x18, Pallas kernels, call(): pl.pallas_call(body, out_shape=outs, in_specs=[VM] * len(ins) if specs is...  29.4 us
    ppermute x9, starting transfers between devices, permute(): return lax.ppermute(x, 'rep', pairs)  17.5 us
    ppermute x9, waiting for transfers between devices, permute(): return lax.ppermute(x, 'rep', pairs)  4.38 us
    unnamed x10, local copies, waits for them, and re-layouts  1.6 us
  transfers between devices with their start and end apart: 9, of which 5 were waited for; matrix products, arithmetic and copies ran while one was open for 0% of the time, Pallas kernels for 52%

profile of v1, /device:TPU:0, one launch (start us, length us, event | category | flops | bytes accessed | tf_op | source)
XLA Modules:
  0.0 53.0 jit_solution(8911954532838559039)
XLA Ops:
  0.0 0.0 copy-start.3
  0.0 0.9 %copy-done.3 = bf16[8,8192]{1,0:T(8,128)(2,1)S(1)} copy-done((bf16[8,8192]{1,0:T(8,128)(2,1)S(1)}, bf16[8,8192]{1,0:T(8,128)(2,1)}, u32[]{:S(2)}) %copy-start.3) | copy-done | bytes 131096
  0.9 0.0 copy-start.4
  0.9 0.7 %copy-done.4 = s32[16,8]{0,1:T(8,128)S(1)} copy-done((s32[16,8]{0,1:T(8,128)S(1)}, s32[16,8]{0,1:T(8,128)}, u32[]{:S(2)}) %copy-start.4) | copy-done | bytes 536
  1.6 0.5 collective-permute-start
  2.1 0.9 %collective-permute-done.r_ref = bf16[8,4096]{1,0:T(8,128)(2,1)S(1)} collective-permute-done((bf16[8,4096]{1,0:T(8,128)(2,1)S(1)}, bf16[8,4096]{1,0:T(8,128)(2,1)S(1)}, u32[]{:S(2)}, u32[]{:S(2)}) %collective-permute-start) | collective-permute-done | bytes 65568 | tf_op jit(solution)/shard_map/ppermute | solution.py:219
  3.1 4.0 %collective-permute-start.1 = (bf16[16,4096]{1,0:T(8,128)(2,1)S(1)}, bf16[16,4096]{1,0:T(8,128)(2,1)S(1)}, u32[]{:S(2)}, u32[]{:S(2)}) collective-permute-start(bf16[16,4096]{1,0:T(8,128)(2,1)S(1)} %shard_map.74.m_ref), channel_id=1, source_target_pairs={{0,8},{1,3},{2,10},{3,1},{4,12},{5,7},{6,14},{7,5},{8,0},{9,11},{1... | collective-permute-start | bytes 393224 | tf_op jit(solution)/shard_map/ppermute | solution.py:219
  7.1 0.4 shard_map.75.v_ref
  7.4 2.1 %shard_map.76.refs_1_ = bf16[1024,1792]{1,0:T(8,128)(2,1)S(1)} custom-call(bf16[8192,1792]{1,0:T(8,128)(2,1)} %refs_5_.7, bf16[8192,1792]{1,0:T(8,128)(2,1)} %refs_6_.7), custom_call_target="tpu_custom_call" | custom-call | bytes 3670016 | tf_op jit(solution)/shard_map/pallas_call | solution.py:32
  9.5 0.5 collective-permute-done.1.r_ref
  10.1 2.5 %collective-permute-start.2 = (bf16[32,4096]{1,0:T(8,128)(2,1)S(1)}, bf16[32,4096]{1,0:T(8,128)(2,1)S(1)}, u32[]{:S(2)}, u32[]{:S(2)}) collective-permute-start(bf16[32,4096]{1,0:T(8,128)(2,1)S(1)} %shard_map.77.m_ref), channel_id=1, source_target_pairs={{0,4},{1,9},{2,6},{3,11},{4,0},{5,13},{6,2},{7,15},{8,12},{9,1},{1... | collective-permute-start | bytes 786440 | tf_op jit(solution)/shard_map/ppermute | solution.py:219
  12.5 5.3 %shard_map.78 = (bf16[1024,1792]{1,0:T(8,128)(2,1)S(1)}, bf16[1024,1792]{1,0:T(8,128)(2,1)S(1)}, bf16[1024,1792]{1,0:T(8,128)(2,1)S(1)}, bf16[1024,1792]{1,0:T(8,128)(2,1)S(1)}) custom-call(bf16[8192,1792]{1,0:T(8,128)(2,1)} %refs_5_.7, bf16[8192,1792]{1,0:T(8,128)(2,1)} %refs_6_.7), custom_call_target="tpu_custom_call" | custom-call | bytes 14680064 | tf_op jit(solution)/shard_map/pallas_call | solution.py:32
  17.9 0.7 %collective-permute-done.2.r_ref = bf16[32,4096]{1,0:T(8,128)(2,1)S(1)} collective-permute-done((bf16[32,4096]{1,0:T(8,128)(2,1)S(1)}, bf16[32,4096]{1,0:T(8,128)(2,1)S(1)}, u32[]{:S(2)}, u32[]{:S(2)}) %collective-permute-start.2) | collective-permute-done | bytes 262176 | tf_op jit(solution)/shard_map/ppermute | solution.py:219
  18.5 0.1 shard_map.79.m_ref
  18.6 0.0 copy-start.2
  18.6 3.0 %collective-permute-start.3 = (bf16[64,4096]{1,0:T(8,128)(2,1)S(1)}, bf16[64,4096]{1,0:T(8,128)(2,1)S(1)}, u32[]{:S(2)}, u32[]{:S(2)}) collective-permute-start(bf16[64,4096]{1,0:T(8,128)(2,1)S(1)} %shard_map.79.m_ref), channel_id=1, source_target_pairs={{0,2},{1,5},{2,0},{3,7},{4,6},{5,1},{6,4},{7,3},{8,10},{9,13},{10,... | collective-permute-start | bytes 1572872 | tf_op jit(solution)/shard_map/ppermute | solution.py:219
  21.6 5.3 %shard_map.80 = (bf16[1024,1792]{1,0:T(8,128)(2,1)S(1)}, bf16[1024,1792]{1,0:T(8,128)(2,1)S(1)}, bf16[1024,1792]{1,0:T(8,128)(2,1)S(1)}, bf16[1024,1792]{1,0:T(8,128)(2,1)S(1)}) custom-call(bf16[8192,1792]{1,0:T(8,128)(2,1)} %refs_5_.7, bf16[8192,1792]{1,0:T(8,128)(2,1)} %refs_6_.7), custom_call_target="tpu_custom_call" | custom-call | bytes 14680064 | tf_op jit(solution)/shard_map/pallas_call | solution.py:32
  26.9 1.8 %collective-permute-done.3.r_ref = bf16[64,4096]{1,0:T(8,128)(2,1)S(1)} collective-permute-done((bf16[64,4096]{1,0:T(8,128)(2,1)S(1)}, bf16[64,4096]{1,0:T(8,128)(2,1)S(1)}, u32[]{:S(2)}, u32[]{:S(2)}) %collective-permute-start.3) | collective-permute-done | bytes 524320 | tf_op jit(solution)/shard_map/ppermute | solution.py:219
  28.8 0.1 shard_map.81.x_ref.refs_0_
  28.8 0.1 collective-permute-start.4
  28.9 0.0 copy-done.2
  28.9 0.4 shard_map.82.a_ref
  29.4 0.6 %collective-permute-start.5 = (f32[128,128]{1,0:T(8,128)S(1)}, f32[128,128]{1,0:T(8,128)S(1)}, u32[]{:S(2)}, u32[]{:S(2)}) collective-permute-start(f32[128,128]{1,0:T(8,128)S(1)} %shard_map.82.a_ref), channel_id=1, source_target_pairs={{0,1},{1,0},{2,3},{3,2},{4,5},{5,4},{6,7},{7,6},{8,9},{9,8},{10,11... | collective-permute-start | bytes 196616 | tf_op jit(solution)/shard_map/ppermute | solution.py:219
  29.9 4.2 %shard_map.83 = (f32[128,1792]{1,0:T(8,128)S(1)}, f32[128,1792]{1,0:T(8,128)S(1)}, bf16[1024,1792]{1,0:T(8,128)(2,1)S(1)}, bf16[1024,1792]{1,0:T(8,128)(2,1)S(1)}, bf16[1024,1792]{1,0:T(8,128)(2,1)S(1)}) custom-call(bf16[128,4096]{1,0:T(8,128)(2,1)S(1)} %shard_map.81.x_ref.refs_0_, bf16[1024,1792]{1,0:T(8,128)(2,1)S(1)} %shard_map.76.refs_1_, ...), custom_call_target="tpu_custom_call" | custom-call | flops 1879048192 | bytes 14680064 | tf_op jit(solution)/shard_map/pallas_call | solution.py:32
  34.2 0.0 collective-permute-done.5.b_ref
  34.2 2.7 %collective-permute-start.6 = (f32[128,128]{1,0:T(8,128)S(1)}, f32[128,128]{1,0:T(8,128)S(1)}, u32[]{:S(2)}, u32[]{:S(2)}) collective-permute-start(f32[128,128]{1,0:T(8,128)S(1)} %shard_map.85.a_ref), channel_id=1, source_target_pairs={{0,8},{1,9},{2,10},{3,11},{4,12},{5,13},{6,14},{7,15},{8,0},{9,1},... | collective-permute-start | bytes 196616 | tf_op jit(solution)/shard_map/ppermute | solution.py:219
  36.9 5.3 %shard_map.84 = (f32[128,1792]{1,0:T(8,128)S(1)}, f32[128,1792]{1,0:T(8,128)S(1)}, bf16[1024,1792]{1,0:T(8,128)(2,1)S(1)}, bf16[1024,1792]{1,0:T(8,128)(2,1)S(1)...) custom-call(bf16[128,4096]{1,0:T(8,128)(2,1)S(1)} %shard_map.81.x_re, ...), custom_call_target="tpu_custom_call", output_to_operand_aliasing={{0}: (7, {}), {1}: (8, {})} | custom-call | flops 1879048192 | bytes 14680064 | tf_op jit(solution)/shard_map/pallas_call | solution.py:32
  42.2 0.0 collective-permute-done.6.b_ref
  42.2 2.6 %collective-permute-start.7 = (f32[128,128]{1,0:T(8,128)S(1)}, f32[128,128]{1,0:T(8,128)S(1)}, u32[]{:S(2)}, u32[]{:S(2)}) collective-permute-start(f32[128,128]{1,0:T(8,128)S(1)} %shard_map.86.a_ref), channel_id=1, source_target_pairs={{0,4},{1,5},{2,6},{3,7},{4,0},{5,1},{6,2},{7,3},{8,12},{9,13},{10,... | collective-permute-start | bytes 196616 | tf_op jit(solution)/shard_map/ppermute | solution.py:219
  44.9 0.0 collective-permute-done.4.refs_0_
  44.9 2.3 %shard_map.87 = (f32[128,1792]{1,0:T(8,128)S(1)}, f32[128,1792]{1,0:T(8,128)S(1)}) custom-call(bf16[128,4096]{1,0:T(8,128)(2,1)S(1)} %collective-permute-done.4.refs_0_, bf16[1024,1792]{1,0:T(8,128)(2,1)S(1)} %get-tuple-element.71.refs_1_, bf16[1024,1792]{1,0:T(8,128)(2,1)S(1)} %get-tuple-element.72.refs_2_, ...), custom_call_target="tpu_custom_call", output_to_operand_aliasing={{0}: (7, {}), {1}: (8, {})} | custom-call | flops 1879048192 | bytes 14680064 | tf_op jit(solution)/shard_map/pallas_call | solution.py:32
  47.2 0.0 collective-permute-done.7.b_ref
  47.2 1.6 %collective-permute-start.8 = (f32[128,128]{1,0:T(8,128)S(1)}, f32[128,128]{1,0:T(8,128)S(1)}, u32[]{:S(2)}, u32[]{:S(2)}) collective-permute-start(f32[128,128]{1,0:T(8,128)S(1)} %shard_map.89.s_ref), channel_id=1, source_target_pairs={{0,2},{1,3},{2,0},{3,1},{4,6},{5,7},{6,4},{7,5},{8,10},{9,11},{10,... | collective-permute-start | bytes 196616 | tf_op jit(solution)/shard_map/ppermute | solution.py:219
  48.8 0.0 copy-start
  48.8 0.0 copy-start.1
  48.8 2.3 %shard_map.88 = (f32[128,1792]{1,0:T(8,128)S(1)}, f32[128,1792]{1,0:T(8,128)S(1)}) custom-call(bf16[128,4096]{1,0:T(8,128)(2,1)S(1)} %collective-permute-done.4.refs_0_, bf16[1024,1792]{1,0:T(8,128)(2,1)S(1)} %get-tuple-element.64.refs_1_, bf16[1024,1792]{1,0:T(8,128)(2,1)S(1)} %get-tuple-element.65.refs_2_, ...), custom_call_target="tpu_custom_call", output_to_operand_aliasing={{0}: (7, {}), {1}: (8, {})} | custom-call | flops 1879048192 | bytes 14680064 | tf_op jit(solution)/shard_map/pallas_call | solution.py:32
  51.1 0.4 collective-permute-done.8.r_ref
  51.5 0.0 copy-done
  51.5 0.0 copy-done.1
  51.5 1.5 %shard_map.90 = bf16[128,1792]{1,0:T(8,128)(2,1)} custom-call(f32[128,1792]{1,0:T(8,128)S(1)} %get-tuple-element.80.tg_ref, f32[128,1792]{1,0:T(8,128)S(1)} %get-tuple-element.81.tu_ref, f32[128,128]{1,0:T(8,128)S(1)} %shard_map.89.s_ref, f32[128,128]{1,0:T(8,128)S(1)} %collective-permute-done.8.r_ref, s32[128,128]{1,0:T(8,128)S(1)} %shard_map.75.v_ref, ...), custom_call_target="tpu_custom_call" | custom-call | tf_op jit(solution)/shard_map/pallas_call | solution.py:32
  (6 shorter events, 0.1 us)
Async XLA Ops:
  0.0 0.9 %copy-start.3 = (bf16[8,8192]{1,0:T(8,128)(2,1)S(1)}, bf16[8,8192]{1,0:T(8,128)(2,1)}, u32[]{:S(2)}) copy-start(bf16[8,8192]{1,0:T(8,128)(2,1)} %x_ref.1) | copy-start | bytes 393220
  0.9 0.7 %copy-start.4 = (s32[16,8]{0,1:T(8,128)S(1)}, s32[16,8]{0,1:T(8,128)}, u32[]{:S(2)}) copy-start(s32[16,8]{0,1:T(8,128)} %param.8) | copy-start | bytes 1540
  1.6 1.4 %collective-permute-start = (bf16[8,4096]{1,0:T(8,128)(2,1)S(1)}, bf16[8,4096]{1,0:T(8,128)(2,1)S(1)}, u32[]{:S(2)}, u32[]{:S(2)}) collective-permute-start(bf16[8,4096]{1,0:T(8,128)(2,1)S(1)} %get-tuple-element.45), channel_id=1, source_target_pairs={{0,1},{1,0},{2,3},{3,2},{4,5},{5,4},{6,7},{7,6},{8,9},{9,8},{10,11... | collective-permute-start | bytes 196616 | tf_op jit(solution)/shard_map/ppermute | solution.py:219
  3.1 7.0 %collective-permute-start.1 = (bf16[16,4096]{1,0:T(8,128)(2,1)S(1)}, bf16[16,4096]{1,0:T(8,128)(2,1)S(1)}, u32[]{:S(2)}, u32[]{:S(2)}) collective-permute-start(bf16[16,4096]{1,0:T(8,128)(2,1)S(1)} %shard_map.74.m_ref), channel_id=1, source_target_pairs={{0,8},{1,3},{2,10},{3,1},{4,12},{5,7},{6,14},{7,5},{8,0},{9,11},{1... | collective-permute-start | bytes 393224 | tf_op jit(solution)/shard_map/ppermute | solution.py:219
  10.1 8.5 %collective-permute-start.2 = (bf16[32,4096]{1,0:T(8,128)(2,1)S(1)}, bf16[32,4096]{1,0:T(8,128)(2,1)S(1)}, u32[]{:S(2)}, u32[]{:S(2)}) collective-permute-start(bf16[32,4096]{1,0:T(8,128)(2,1)S(1)} %shard_map.77.m_ref), channel_id=1, source_target_pairs={{0,4},{1,9},{2,6},{3,11},{4,0},{5,13},{6,2},{7,15},{8,12},{9,1},{1... | collective-permute-start | bytes 786440 | tf_op jit(solution)/shard_map/ppermute | solution.py:219
  18.6 10.3 %copy-start.2 = (bf16[8,512,128]{2,1,0:T(8,128)(2,1)S(1)}, bf16[8,512,128]{2,1,0:T(8,128)(2,1)}, u32[]{:S(2)}) copy-start(bf16[8,512,128]{2,1,0:T(8,128)(2,1)} %d_ref.1) | copy-start | bytes 3145732
  18.6 10.1 %collective-permute-start.3 = (bf16[64,4096]{1,0:T(8,128)(2,1)S(1)}, bf16[64,4096]{1,0:T(8,128)(2,1)S(1)}, u32[]{:S(2)}, u32[]{:S(2)}) collective-permute-start(bf16[64,4096]{1,0:T(8,128)(2,1)S(1)} %shard_map.79.m_ref), channel_id=1, source_target_pairs={{0,2},{1,5},{2,0},{3,7},{4,6},{5,1},{6,4},{7,3},{8,10},{9,13},{10,... | collective-permute-start | bytes 1572872 | tf_op jit(solution)/shard_map/ppermute | solution.py:219
  28.8 16.0 %collective-permute-start.4 = (bf16[128,4096]{1,0:T(8,128)(2,1)S(1)}, bf16[128,4096]{1,0:T(8,128)(2,1)S(1)}, u32[]{:S(2)}, u32[]{:S(2)}) collective-permute-start(bf16[128,4096]{1,0:T(8,128)(2,1)S(1)} %shard_map.81.x_ref.refs_0_), channel_id=1, source_target_pairs={{0,1},{1,0},{2,3},{3,2},{4,5},{5,4},{6,7},{7,6},{8,9},{9,8},{10,11... | collective-permute-start | bytes 3145736 | tf_op jit(solution)/shard_map/ppermute | solution.py:219
  29.4 4.8 %collective-permute-start.5 = (f32[128,128]{1,0:T(8,128)S(1)}, f32[128,128]{1,0:T(8,128)S(1)}, u32[]{:S(2)}, u32[]{:S(2)}) collective-permute-start(f32[128,128]{1,0:T(8,128)S(1)} %shard_map.82.a_ref), channel_id=1, source_target_pairs={{0,1},{1,0},{2,3},{3,2},{4,5},{5,4},{6,7},{7,6},{8,9},{9,8},{10,11... | collective-permute-start | bytes 196616 | tf_op jit(solution)/shard_map/ppermute | solution.py:219
  34.2 8.0 %collective-permute-start.6 = (f32[128,128]{1,0:T(8,128)S(1)}, f32[128,128]{1,0:T(8,128)S(1)}, u32[]{:S(2)}, u32[]{:S(2)}) collective-permute-start(f32[128,128]{1,0:T(8,128)S(1)} %shard_map.85.a_ref), channel_id=1, source_target_pairs={{0,8},{1,9},{2,10},{3,11},{4,12},{5,13},{6,14},{7,15},{8,0},{9,1},... | collective-permute-start | bytes 196616 | tf_op jit(solution)/shard_map/ppermute | solution.py:219
  42.2 4.9 %collective-permute-start.7 = (f32[128,128]{1,0:T(8,128)S(1)}, f32[128,128]{1,0:T(8,128)S(1)}, u32[]{:S(2)}, u32[]{:S(2)}) collective-permute-start(f32[128,128]{1,0:T(8,128)S(1)} %shard_map.86.a_ref), channel_id=1, source_target_pairs={{0,4},{1,5},{2,6},{3,7},{4,0},{5,1},{6,2},{7,3},{8,12},{9,13},{10,... | collective-permute-start | bytes 196616 | tf_op jit(solution)/shard_map/ppermute | solution.py:219
  47.2 4.3 %collective-permute-start.8 = (f32[128,128]{1,0:T(8,128)S(1)}, f32[128,128]{1,0:T(8,128)S(1)}, u32[]{:S(2)}, u32[]{:S(2)}) collective-permute-start(f32[128,128]{1,0:T(8,128)S(1)} %shard_map.89.s_ref), channel_id=1, source_target_pairs={{0,2},{1,3},{2,0},{3,1},{4,6},{5,7},{6,4},{7,5},{8,10},{9,11},{10,... | collective-permute-start | bytes 196616 | tf_op jit(solution)/shard_map/ppermute | solution.py:219
  48.8 2.7 %copy-start = (bf16[8,64,1792]{2,1,0:T(8,128)(2,1)S(1)}, bf16[8,64,1792]{2,1,0:T(8,128)(2,1)}, u32[]{:S(2)}) copy-start(bf16[8,64,1792]{2,1,0:T(8,128)(2,1)} %param.12) | copy-start | bytes 5505028
  48.8 2.7 %copy-start.1 = (bf16[8,64,1792]{2,1,0:T(8,128)(2,1)S(1)}, bf16[8,64,1792]{2,1,0:T(8,128)(2,1)}, u32[]{:S(2)}) copy-start(bf16[8,64,1792]{2,1,0:T(8,128)(2,1)} %param.13) | copy-start | bytes 5505028

commit v2 on v0

--- a/solution.py
+++ b/solution.py
@@ -1,14 +1,260 @@
+import functools
+
 import jax
 import jax.numpy as jnp
 from jax import lax
+from jax.experimental import pallas as pl
+from jax.experimental.pallas import tpu as pltpu
 from jax.sharding import PartitionSpec as P
 
 ADAPTER_RANK = 64
 POLICY_VERSIONS = 8
 ROWS_DEV = 8
-
-
 adapter_scale = 2.0
+
+F32, BF16 = jnp.float32, jnp.bfloat16
+MiB = 2**20
+VM = pl.BlockSpec(memory_space=pltpu.VMEM)
+HB = pl.BlockSpec(memory_space=pltpu.HBM)
+
+LANE_BITS = ((4, 2, 1), (1, 4, 2))
+SUM_BITS = (1, 2, 4)
+UNIT = 1024
+EARLY = (1, 4, 5)
+LATE = (2, 2, 2, 0)
+
+
+def dot(a, b):
+    return jnp.dot(a, b, preferred_element_type=F32)
+
+
+def place():
+    me = lax.axis_index("rep")
+    return me // 2, lax.rem(me, 2)
+
+
+def chip_of(core, spot):
+    return sum(bit * ((spot >> k) & 1) for k, bit in enumerate(LANE_BITS[core]))
+
+
+def like(shape, dtype=BF16):
+    return jax.ShapeDtypeStruct(shape, dtype)
+
+
+def call(body, outs, ins, specs=None, scratch=(), vmem=2, bytes_=0, flops=0, alias=None):
+    return pl.pallas_call(
+        body,
+        out_shape=outs,
+        in_specs=[VM] * len(ins) if specs is None else specs,
+        out_specs=jax.tree.map(lambda _: VM, outs),
+        scratch_shapes=list(scratch),
+        input_output_aliases=alias or {},
+        compiler_params=pltpu.CompilerParams(vmem_limit_bytes=int(vmem * MiB)),
+        cost_estimate=pl.CostEstimate(flops=int(flops), bytes_accessed=int(bytes_), transcendentals=0),
+    )(*ins)
+
+
+def double(step, m_ref, r_ref, o_ref):
+    chip, core = place()
+    rows = m_ref.shape[0]
+    bit = jnp.where(core == 0, lax.rem(chip // LANE_BITS[0][step], 2), lax.rem(chip // LANE_BITS[1][step], 2))
+    if step == 0:
+        mine, other = m_ref[...], r_ref[...]
+        first = jnp.where(bit == 0, mine, other)
+        second = jnp.where(bit == 0, other, mine)
+        o_ref[...] = jnp.concatenate([first, second], axis=0)
+    else:
+        o_ref[pl.ds(pl.multiple_of(bit * rows, rows), rows), :] = m_ref[...]
+        o_ref[pl.ds(pl.multiple_of((1 - bit) * rows, rows), rows), :] = r_ref[...]
+
+
+def join(m_ref, r_ref, o_ref):
+    _, core = place()
+    rows = m_ref.shape[0]
+    o_ref[pl.ds(pl.multiple_of(core * rows, rows), rows), :] = m_ref[...]
+    o_ref[pl.ds(pl.multiple_of((1 - core) * rows, rows), rows), :] = r_ref[...]
+
+
+def versions(c_ref, o_ref):
+    rows, reps = o_ref.shape[0], c_ref.shape[1]
+    row = lax.broadcasted_iota(jnp.int32, (rows, reps), 0)
+    group = row // ROWS_DEV
+    spot, core = lax.rem(group, 8), group // 8
+    chip = jnp.where(core == 0, chip_of(0, spot), chip_of(1, spot))
+    holds = (2 * chip + core == lax.broadcasted_iota(jnp.int32, (rows, reps), 1)).astype(F32)
+    counts = lax.dot_general(holds, c_ref[...].astype(F32), (((1,), (1,)), ((), ())), preferred_element_type=F32)
+    spot = lax.rem(lax.broadcasted_iota(jnp.int32, (rows, 1), 0), ROWS_DEV).astype(F32)
+    running = jnp.zeros_like(spot)
+    version = jnp.zeros((rows, 1), jnp.int32)
+    for v in range(POLICY_VERSIONS):
+        running = running + counts[:, v : v + 1]
+        version = version + (running <= spot).astype(jnp.int32)
+    o_ref[...] = jnp.broadcast_to(version, o_ref.shape)
+
+
+def partial(x_ref, d_ref, e_ref, v_ref, o_ref):
+    chip, core = place()
+    feats = d_ref.shape[1]
+    mine = x_ref[:, pl.ds(pl.multiple_of((2 * chip + core) * feats, feats), feats)]
+    other = x_ref[:, pl.ds(pl.multiple_of((2 * chip + 1 - core) * feats, feats), feats)]
+    rows = x_ref.shape[0]
+    version = v_ref[pl.ds(pl.multiple_of(core * rows, rows), rows), :]
+    total = jnp.zeros(o_ref.shape, F32)
+    for v in range(POLICY_VERSIONS):
+        total = total + jnp.where(version == v, dot(mine, d_ref[v]) + dot(other, e_ref[v]), 0.0)
+    o_ref[...] = total
+
+
+def add(*refs):
+    total = refs[0][...]
+    for ref in refs[1:-1]:
+        total = total + ref[...]
+    refs[-1][...] = total
+
+
+def finish(tg_ref, tu_ref, s_ref, r_ref, v_ref, ag_ref, au_ref, o_ref):
+    _, core = place()
+    mine, other = s_ref[...], r_ref[...]
+    shrink = jnp.concatenate([jnp.where(core == 0, mine, other), jnp.where(core == 0, other, mine)], axis=0)
+    turned = pltpu.roll(shrink, ADAPTER_RANK, 1)
+    column = lax.broadcasted_iota(jnp.int32, shrink.shape, 1)
+    low = column < ADAPTER_RANK
+    version = v_ref[...]
+    half = (column >= ADAPTER_RANK).astype(jnp.int32)
+    wide = []
+    for twice in (jnp.where(low, shrink, turned), jnp.where(low, turned, shrink)):
+        parts = [jnp.where(version == 2 * k + half, twice, 0.0).astype(BF16) for k in range(POLICY_VERSIONS // 2)]
+        wide.append(jnp.concatenate(parts, axis=1))
+    groups = shrink.shape[0] // ROWS_DEV
+    where = {}
+    for core_ in range(2):
+        for spot in range(groups // 2):
+            where[2 * chip_of(core_, spot) + core_] = (core_ * (groups // 2) + spot) * ROWS_DEV
+    for n in range(0, o_ref.shape[1], 256):
+        gate = tg_ref[:, n : n + 256] + adapter_scale * dot(wide[0], ag_ref[:, n : n + 256])
+        up = tu_ref[:, n : n + 256] + adapter_scale * dot(wide[1], au_ref[:, n : n + 256])
+        hidden = gate / (1.0 + jnp.exp(-gate)) * up
+        for r in range(0, groups, 2):
+            two = [hidden[where[k] : where[k] + ROWS_DEV] for k in (r, r + 1)]
+            o_ref[r * ROWS_DEV : (r + 2) * ROWS_DEV, n : n + 256] = jnp.concatenate(two, axis=0).astype(BF16)
+
+
+def work(todo, x, have, units, hbm, totals):
+    cols = hbm[0].shape[1]
+    done = sorted({m for m, _ in todo})
+    old = [m for m in done if totals[m] is not None]
+    nt, nu = len(todo), len(units)
+
+    def body(*refs):
+        refs = list(refs)
+
+        def take(n):
+            got, refs[:] = refs[:n], refs[n:]
+            return got
+
+        x_refs, w_refs, hbm_refs = take(1 if nt else 0), take(nt), take(2)
+        old_refs, new_refs = dict(zip(old, take(len(old)))), dict(zip(done, take(len(done))))
+        copies = [
+            pltpu.make_async_copy(
+                hbm_refs[m].at[pl.ds(k * UNIT + h * UNIT // 2, UNIT // 2), :], to_ref.at[pl.ds(h * UNIT // 2, UNIT // 2), :], refs[nu].at[2 * i + h]
+            )
+            for i, ((m, k), to_ref) in enumerate(zip(units, refs[:nu]))
+            for h in range(2)
+        ]
+        for c in copies:
+            c.start()
+
+        @pl.when(lax.axis_index("rep") >= 0)
+        def _():
+            for m in done:
+                for n in range(0, cols, 256):
+                    total = old_refs[m][:, n : n + 256] if m in old_refs else None
+                    for (m2, k), w_ref in zip(todo, w_refs):
+                        if m2 == m:
+                            term = dot(x_refs[0][:, k * UNIT : (k + 1) * UNIT], w_ref[:, n : n + 256])
+                            total = term if total is None else total + term
+                    new_refs[m][:, n : n + 256] = total
+
+        for c in copies:
+            c.wait()
+
+    ins = ([x] if nt else []) + [have[t] for t in todo]
+    specs = [VM] * len(ins) + [HB] * 2 + [VM] * len(old)
+    ins += hbm
+    alias = {len(ins) + i: done.index(m) for i, m in enumerate(old)}
+    ins += [totals[m] for m in old]
+    rows = x.shape[0] if nt else 0
+    outs = [like((rows, cols), F32) for _ in done] + [like((UNIT, cols)) for _ in units]
+    got = call(
+        body, outs, ins, specs, [pltpu.SemaphoreType.DMA((2 * nu,))] if nu else [], vmem=4, alias=alias,
+        bytes_=UNIT * cols * 2 * max(nt, nu), flops=2 * rows * UNIT * cols * nt,
+    )
+    for m, t in zip(done, got):
+        totals[m] = t
+    for unit, w in zip(units, got[len(done) :]):
+        have[unit] = pltpu.with_memory_space_constraint(w, pltpu.VMEM)
+
+
+def cores():
+    return [(i, i ^ 1) for i in range(16)]
+
+
+def lanes(step):
+    return [(2 * c + k, 2 * (c ^ LANE_BITS[k][step]) + k) for c in range(8) for k in range(2)]
+
+
+def chips(bits):
+    return [(i, i ^ (2 * bits)) for i in range(16)]
+
+
+def permute(x, pairs):
+    return lax.ppermute(x, "rep", pairs)
+
+
+def split(items, sizes):
+    return [items[sum(sizes[:i]) : sum(sizes[: i + 1])] for i in range(len(sizes))]
+
+
+def hold(*values):
+    return lax.optimization_barrier(values)
+
+
+def tuned(x, counts, g, u, down, ag, au):
+    feats, cols = g.shape
+    hbm = [pltpu.with_memory_space_constraint(w, pltpu.HBM) for w in (g, u)]
+    rows = counts.shape[0] * ROWS_DEV
+    order = [(m, k) for k in range(feats // UNIT) for m in range(2)]
+    early = split(order, EARLY)
+    late = split(order[sum(EARLY) :], LATE)
+    have, totals = {}, [None, None]
+    a = x
+    for step in range(3):
+        r = permute(a, lanes(step))
+        if step == 0:
+            e = permute(down, cores())
+            version = call(versions, like((rows, 128), jnp.int32), (counts.T,))
+        work([], None, have, early[step], hbm, totals)
+        last = early[step][-1]
+        if step == 0:
+            r, version, have[last] = hold(r, version, have[last])
+        else:
+            r, have[last] = hold(r, have[last])
+        a = call(functools.partial(double, step), like((a.shape[0] * 2, feats)), (a, r))
+    other = permute(a, cores())
+    part = call(partial, like((rows // 2, 128), F32), (a, down, e, version))
+    got = permute(part, chips(SUM_BITS[0]))
+    x = call(join, like((rows, feats)), (a, other))
+    per = len(order) // 4
+    for j in range(4):
+        work(order[per * j : per * (j + 1)], x, have, late[j], hbm, totals)
+        if j < 3:
+            got, totals[0] = hold(got, totals[0])
+            part = call(add, like((rows // 2, 128), F32), (part, got))
+            got = permute(part, chips(SUM_BITS[j + 1]) if j < 2 else cores())
+    wide = POLICY_VERSIONS * ADAPTER_RANK
+    return call(
+        finish, like((rows, cols)), (*totals, part, got, version, ag.reshape(wide, cols), au.reshape(wide, cols)), vmem=6
+    )
 
 
 def row_versions(counts):
@@ -24,7 +270,7 @@
     return widened.reshape(total_rows, POLICY_VERSIONS * ADAPTER_RANK).astype(jnp.bfloat16)
 
 
-def local(
+def general(
     normed_input_rows,
     counts,
     gate_weight_matrix,
@@ -75,6 +321,5 @@
         P("groups", None, "rep"),
         P("groups", None, "rep"),
     )
-    return jax.shard_map(
-        local, mesh=mesh, in_specs=placed, out_specs=P("groups", "rep"), check_vma=False
-    )
+    local = tuned if mesh.shape["rep"] == 16 else general
+    return jax.shard_map(local, mesh=mesh, in_specs=placed, out_specs=P("groups", "rep"), check_vma=False)

time: 149 us -> 48.1 us (0.32)
  blocking collectives: 59.6 us -> 0 us
  waiting for transfers between devices: 46.2 us -> 2.26 us
  Pallas kernels: 0 us -> 28.4 us
  matrix products: 27.7 us -> 0 us
  starting transfers between devices: 0.01 us -> 16.4 us
  between operations: 13.5 us -> 0.21 us
    psum x1 -> x0, blocking collectives: 59.6 us -> none  [local(): lax.psum(combined_down[:, 2 * hidden_local:], 'rep').astype(jnp.bfloat16)]
    all_gather x1 -> x0, waiting for transfers between devices: 45.5 us -> none  [local(): piece = lax.all_gather(normed_input_rows, 'rep', axis=0, tiled=True)]
    pallas_call x0 -> x17, Pallas kernels: none -> 28.4 us  [call(): pl.pallas_call(body, out_shape=outs, in_specs=[VM] * len(ins) if specs is...]
    dot_general x5 -> x0, matrix products: 27.7 us -> none  [the longest x1 12.3 us: local(): jnp.dot(piece, gate_weight_matrix, preferred_element_type=jnp.float32)]
    ppermute x0 -> x9, starting transfers between devices: none -> 16.4 us  [permute(): return lax.ppermute(x, 'rep', pairs)]
    ppermute x0 -> x9, waiting for transfers between devices: none -> 2.26 us  [permute(): return lax.ppermute(x, 'rep', pairs)]
  transfers between devices with their start and end apart: 1 -> 9, of which waited for: 1 -> 4; matrix products, arithmetic and copies ran while one was open for 1% -> 0% of each run, Pallas kernels for 0% -> 56%
where the time goes in v2:
time: 48.1 us; the launch traced here: 48 us
  Pallas kernels  28.4 us (59%)
  starting transfers between devices  16.4 us (34%)
  waiting for transfers between devices  2.26 us (5%)
  local copies, waits for them, and re-layouts  0.71 us (1%)
    pallas_call x17, Pallas kernels, call(): pl.pallas_call(body, out_shape=outs, in_specs=[VM] * len(ins) if specs is...  28.4 us
    ppermute x9, starting transfers between devices, permute(): return lax.ppermute(x, 'rep', pairs)  16.4 us
    ppermute x9, waiting for transfers between devices, permute(): return lax.ppermute(x, 'rep', pairs)  2.26 us
  transfers between devices with their start and end apart: 9, of which 4 were waited for; matrix products, arithmetic and copies ran while one was open for 0% of the time, Pallas kernels for 56%

profile of v2, /device:TPU:0, one launch (start us, length us, event | category | flops | bytes accessed | tf_op | source)
XLA Modules:
  0.0 48.0 jit_solution(372928184494657965)
XLA Ops:
  0.0 4.0 %collective-permute-start = (bf16[8,8192]{1,0:T(8,128)(2,1)}, bf16[8,8192]{1,0:T(8,128)(2,1)S(1)}, u32[]{:S(2)}, u32[]{:S(2)}) collective-permute-start(bf16[8,8192]{1,0:T(8,128)(2,1)} %m_ref.1), channel_id=1, source_target_pairs={{0,8},{1,3},{2,10},{3,1},{4,12},{5,7},{6,14},{7,5},{8,0},{9,11},{1... | collective-permute-start | bytes 393224 | tf_op jit(solution)/shard_map/ppermute | solution.py:211
  4.0 0.0 copy-start.4
  4.0 0.7 %copy-done.4 = s32[16,8]{0,1:T(8,128)S(1)} copy-done((s32[16,8]{0,1:T(8,128)S(1)}, s32[16,8]{0,1:T(8,128)}, u32[]{:S(2)}) %copy-start.4) | copy-done | bytes 536
  4.7 0.4 shard_map.73.v_ref
  5.1 0.0 copy-start.3
  5.1 2.1 %shard_map.74.refs_1_ = bf16[1024,1792]{1,0:T(8,128)(2,1)S(1)} custom-call(bf16[8192,1792]{1,0:T(8,128)(2,1)} %refs_5_.7, bf16[8192,1792]{1,0:T(8,128)(2,1)} %refs_6_.7), custom_call_target="tpu_custom_call" | custom-call | bytes 3670016 | tf_op jit(solution)/shard_map/pallas_call | solution.py:45
  7.2 0.0 collective-permute-done.r_ref
  7.2 0.0 copy-done.3
  7.2 0.1 shard_map.75.m_ref
  7.3 0.0 copy-start.2
  7.3 2.5 %collective-permute-start.1 = (bf16[16,8192]{1,0:T(8,128)(2,1)S(1)}, bf16[16,8192]{1,0:T(8,128)(2,1)S(1)}, u32[]{:S(2)}, u32[]{:S(2)}) collective-permute-start(bf16[16,8192]{1,0:T(8,128)(2,1)S(1)} %shard_map.75.m_ref), channel_id=1, source_target_pairs={{0,4},{1,9},{2,6},{3,11},{4,0},{5,13},{6,2},{7,15},{8,12},{9,1},{1... | collective-permute-start | bytes 786440 | tf_op jit(solution)/shard_map/ppermute | solution.py:211
  9.8 5.3 %shard_map.76 = (bf16[1024,1792]{1,0:T(8,128)(2,1)S(1)}, bf16[1024,1792]{1,0:T(8,128)(2,1)S(1)}, bf16[1024,1792]{1,0:T(8,128)(2,1)S(1)}, bf16[1024,1792]{1,0:T(8,128)(2,1)S(1)}) custom-call(bf16[8192,1792]{1,0:T(8,128)(2,1)} %refs_5_.7, bf16[8192,1792]{1,0:T(8,128)(2,1)} %refs_6_.7), custom_call_target="tpu_custom_call" | custom-call | bytes 14680064 | tf_op jit(solution)/shard_map/pallas_call | solution.py:45
  15.2 0.7 %collective-permute-done.1.r_ref = bf16[16,8192]{1,0:T(8,128)(2,1)S(1)} collective-permute-done((bf16[16,8192]{1,0:T(8,128)(2,1)S(1)}, bf16[16,8192]{1,0:T(8,128)(2,1)S(1)}, u32[]{:S(2)}, u32[]{:S(2)}) %collective-permute-start.1) | collective-permute-done | bytes 262176 | tf_op jit(solution)/shard_map/ppermute | solution.py:211
  15.9 0.1 shard_map.77.m_ref
  16.0 2.8 %collective-permute-start.2 = (bf16[32,8192]{1,0:T(8,128)(2,1)S(1)}, bf16[32,8192]{1,0:T(8,128)(2,1)S(1)}, u32[]{:S(2)}, u32[]{:S(2)}) collective-permute-start(bf16[32,8192]{1,0:T(8,128)(2,1)S(1)} %shard_map.77.m_ref), channel_id=1, source_target_pairs={{0,2},{1,5},{2,0},{3,7},{4,6},{5,1},{6,4},{7,3},{8,10},{9,13},{10,... | collective-permute-start | bytes 1572872 | tf_op jit(solution)/shard_map/ppermute | solution.py:211
  18.8 0.0 copy-done.2
  18.8 0.0 collective-permute-start.4
  18.8 6.4 %shard_map.78 = (bf16[1024,1792]{1,0:T(8,128)(2,1)S(1)}, bf16[1024,1792]{1,0:T(8,128)(2,1)S(1)}, bf16[1024,1792]{1,0:T(8,128)(2,1)S(1)}, bf16[1024,1792]{1,0:T(8,128)(2,1)S(1)}, bf16[1024,1792]{1,0:T(8,128)(2,1)S(1)}) custom-call(bf16[8192,1792]{1,0:T(8,128)(2,1)} %refs_5_.7, bf16[8192,1792]{1,0:T(8,128)(2,1)} %refs_6_.7), custom_call_target="tpu_custom_call" | custom-call | bytes 18350080 | tf_op jit(solution)/shard_map/pallas_call | solution.py:45
  25.2 0.8 %collective-permute-done.2.r_ref = bf16[32,8192]{1,0:T(8,128)(2,1)S(1)} collective-permute-done((bf16[32,8192]{1,0:T(8,128)(2,1)S(1)}, bf16[32,8192]{1,0:T(8,128)(2,1)S(1)}, u32[]{:S(2)}, u32[]{:S(2)}) %collective-permute-start.2) | collective-permute-done | bytes 524320 | tf_op jit(solution)/shard_map/ppermute | solution.py:211
  25.9 0.1 shard_map.79.m_ref.x_ref
  26.1 0.1 collective-permute-start.3
  26.1 0.0 collective-permute-done.4.e_ref
  26.1 0.4 shard_map.81.refs_0_
  26.6 2.1 %collective-permute-start.5 = (f32[64,128]{1,0:T(8,128)S(1)}, f32[64,128]{1,0:T(8,128)S(1)}, u32[]{:S(2)}, u32[]{:S(2)}) collective-permute-start(f32[64,128]{1,0:T(8,128)S(1)} %shard_map.81.refs_0_), channel_id=1, source_target_pairs={{0,2},{1,3},{2,0},{3,1},{4,6},{5,7},{6,4},{7,5},{8,10},{9,11},{10,... | collective-permute-start | bytes 98312 | tf_op jit(solution)/shard_map/ppermute | solution.py:211
  28.7 0.1 collective-permute-done.3.r_ref
  28.8 0.1 shard_map.80.refs_0_
  28.9 3.2 %shard_map.82 = (f32[128,1792]{1,0:T(8,128)S(1)}, f32[128,1792]{1,0:T(8,128)S(1)}, bf16[1024,1792]{1,0:T(8,128)(2,1)S(1)}, bf16[1024,1792]{1,0:T(8,128)(2,1)S(1)}) custom-call(bf16[128,8192]{1,0:T(8,128)(2,1)S(1)} %shard_map.80.refs_0_, bf16[1024,1792]{1,0:T(8,128)(2,1)S(1)} %shard_map.74.refs_1_, bf16[1024,1792]{1,0:T(8,128)(2,1)S(1)} %get-tuple-element.52.refs_2_, ...), custom_call_target="tpu_custom_call" | custom-call | flops 1879048192 | bytes 14680064 | tf_op jit(solution)/shard_map/pallas_call | solution.py:45
  32.1 0.0 collective-permute-done.5.refs_1_
  32.2 0.2 collective-permute-start.6
  32.3 3.2 %shard_map.83 = (f32[128,1792]{1,0:T(8,128)S(1)}, f32[128,1792]{1,0:T(8,128)S(1)}, bf16[1024,1792]{1,0:T(8,128)(2,1)S(1)}, bf16[1024,1792]{1,0:T(8,128)(2,1)S(1)}) custom-call(bf16[128,8192]{1,0:T(8,128)(2,1)S(1)} %shard_map.80.refs_0_, bf16[1024,1792]{1,0:T(8,128)(2,1)S(1)} %get-tuple-element.46.refs_1_, ...), custom_call_target="tpu_custom_call", output_to_operand_aliasing={{0}: (7, {}), {1}: (8, {})} | custom-call | flops 1879048192 | bytes 14680064 | tf_op jit(solution)/shard_map/pallas_call | solution.py:45
  35.5 0.6 %collective-permute-done.6.refs_1_ = f32[64,128]{1,0:T(8,128)S(1)} collective-permute-done((f32[64,128]{1,0:T(8,128)S(1)}, f32[64,128]{1,0:T(8,128)S(1)}, u32[]{:S(2)}, u32[]{:S(2)}) %collective-permute-start.6) | collective-permute-done | bytes 32800 | tf_op jit(solution)/shard_map/ppermute | solution.py:211
  36.1 4.6 %collective-permute-start.7 = (f32[64,128]{1,0:T(8,128)S(1)}, f32[64,128]{1,0:T(8,128)S(1)}, u32[]{:S(2)}, u32[]{:S(2)}) collective-permute-start(f32[64,128]{1,0:T(8,128)S(1)} %shard_map.86.refs_0_), channel_id=1, source_target_pairs={{0,8},{1,9},{2,10},{3,11},{4,12},{5,13},{6,14},{7,15},{8,0},{9,1},... | collective-permute-start | bytes 98312 | tf_op jit(solution)/shard_map/ppermute | solution.py:211
  40.8 3.2 %shard_map.85 = (f32[128,1792]{1,0:T(8,128)S(1)}, f32[128,1792]{1,0:T(8,128)S(1)}, bf16[1024,1792]{1,0:T(8,128)(2,1)S(1)}, bf16[1024,1792]{1,0:T(8,128)(2,1)S(1)}) custom-call(bf16[128,8192]{1,0:T(8,128)(2,1)S(1)} %shard_map.80.refs_0_, bf16[1024,1792]{1,0:T(8,128)(2,1)S(1)} %get-tuple-element.60.refs_1_, ...), custom_call_target="tpu_custom_call", output_to_operand_aliasing={{0}: (7, {}), {1}: (8, {})} | custom-call | flops 1879048192 | bytes 14680064 | tf_op jit(solution)/shard_map/pallas_call | solution.py:45
  44.0 0.0 collective-permute-done.7.refs_1_
  44.0 0.1 collective-permute-start.8
  44.1 0.0 copy-start
  44.1 0.0 copy-start.1
  44.1 2.3 %shard_map.87 = (f32[128,1792]{1,0:T(8,128)S(1)}, f32[128,1792]{1,0:T(8,128)S(1)}) custom-call(bf16[128,8192]{1,0:T(8,128)(2,1)S(1)} %shard_map.80.refs_0_, bf16[1024,1792]{1,0:T(8,128)(2,1)S(1)} %get-tuple-element.58.refs_1_, bf16[1024,1792]{1,0:T(8,128)(2,1)S(1)} %get-tuple-element.59.refs_2_, ...), custom_call_target="tpu_custom_call", output_to_operand_aliasing={{0}: (7, {}), {1}: (8, {})} | custom-call | flops 1879048192 | bytes 14680064 | tf_op jit(solution)/shard_map/pallas_call | solution.py:45
  46.4 0.0 collective-permute-done.8.r_ref
  46.4 0.0 copy-done
  46.4 0.0 copy-done.1
  46.5 1.5 %shard_map.89 = bf16[128,1792]{1,0:T(8,128)(2,1)} custom-call(f32[128,1792]{1,0:T(8,128)S(1)} %get-tuple-element.74.tg_ref, f32[128,1792]{1,0:T(8,128)S(1)} %get-tuple-element.75.tu_ref, f32[64,128]{1,0:T(8,128)S(1)} %shard_map.88.s_ref, f32[64,128]{1,0:T(8,128)S(1)} %collective-permute-done.8.r_ref, s32[128,128]{1,0:T(8,128)S(1)} %shard_map.73.v_ref, ...), custom_call_target="tpu_custom_call" | custom-call | tf_op jit(solution)/shard_map/pallas_call | solution.py:45
  (3 shorter events, 0.0 us)
Async XLA Ops:
  0.0 7.2 %collective-permute-start = (bf16[8,8192]{1,0:T(8,128)(2,1)}, bf16[8,8192]{1,0:T(8,128)(2,1)S(1)}, u32[]{:S(2)}, u32[]{:S(2)}) collective-permute-start(bf16[8,8192]{1,0:T(8,128)(2,1)} %m_ref.1), channel_id=1, source_target_pairs={{0,8},{1,3},{2,10},{3,1},{4,12},{5,7},{6,14},{7,5},{8,0},{9,11},{1... | collective-permute-start | bytes 393224 | tf_op jit(solution)/shard_map/ppermute | solution.py:211
  4.0 0.7 %copy-start.4 = (s32[16,8]{0,1:T(8,128)S(1)}, s32[16,8]{0,1:T(8,128)}, u32[]{:S(2)}) copy-start(s32[16,8]{0,1:T(8,128)} %param.8) | copy-start | bytes 1540
  5.1 2.1 %copy-start.3 = (bf16[8,8192]{1,0:T(8,128)(2,1)S(1)}, bf16[8,8192]{1,0:T(8,128)(2,1)}, u32[]{:S(2)}) copy-start(bf16[8,8192]{1,0:T(8,128)(2,1)} %m_ref.1) | copy-start | bytes 393220
  7.3 11.5 %copy-start.2 = (bf16[8,512,128]{2,1,0:T(8,128)(2,1)S(1)}, bf16[8,512,128]{2,1,0:T(8,128)(2,1)}, u32[]{:S(2)}) copy-start(bf16[8,512,128]{2,1,0:T(8,128)(2,1)} %d_ref.1) | copy-start | bytes 3145732
  7.3 8.6 %collective-permute-start.1 = (bf16[16,8192]{1,0:T(8,128)(2,1)S(1)}, bf16[16,8192]{1,0:T(8,128)(2,1)S(1)}, u32[]{:S(2)}, u32[]{:S(2)}) collective-permute-start(bf16[16,8192]{1,0:T(8,128)(2,1)S(1)} %shard_map.75.m_ref), channel_id=1, source_target_pairs={{0,4},{1,9},{2,6},{3,11},{4,0},{5,13},{6,2},{7,15},{8,12},{9,1},{1... | collective-permute-start | bytes 786440 | tf_op jit(solution)/shard_map/ppermute | solution.py:211
  16.0 10.0 %collective-permute-start.2 = (bf16[32,8192]{1,0:T(8,128)(2,1)S(1)}, bf16[32,8192]{1,0:T(8,128)(2,1)S(1)}, u32[]{:S(2)}, u32[]{:S(2)}) collective-permute-start(bf16[32,8192]{1,0:T(8,128)(2,1)S(1)} %shard_map.77.m_ref), channel_id=1, source_target_pairs={{0,2},{1,5},{2,0},{3,7},{4,6},{5,1},{6,4},{7,3},{8,10},{9,13},{10,... | collective-permute-start | bytes 1572872 | tf_op jit(solution)/shard_map/ppermute | solution.py:211
  18.8 7.3 %collective-permute-start.4 = (bf16[8,512,128]{2,1,0:T(8,128)(2,1)S(1)}, bf16[8,512,128]{2,1,0:T(8,128)(2,1)S(1)}, u32[]{:S(2)}, u32[]{:S(2)}) collective-permute-start(bf16[8,512,128]{2,1,0:T(8,128)(2,1)S(1)} %copy-done.2), channel_id=1, source_target_pairs={{0,1},{1,0},{2,3},{3,2},{4,5},{5,4},{6,7},{7,6},{8,9},{9,8},{10,11... | collective-permute-start | bytes 3145736 | tf_op jit(solution)/shard_map/ppermute | solution.py:211
  26.1 2.7 %collective-permute-start.3 = (bf16[64,8192]{1,0:T(8,128)(2,1)S(1)}, bf16[64,8192]{1,0:T(8,128)(2,1)S(1)}, u32[]{:S(2)}, u32[]{:S(2)}) collective-permute-start(bf16[64,8192]{1,0:T(8,128)(2,1)S(1)} %shard_map.79.m_ref.x_ref), channel_id=1, source_target_pairs={{0,1},{1,0},{2,3},{3,2},{4,5},{5,4},{6,7},{7,6},{8,9},{9,8},{10,11... | collective-permute-start | bytes 3145736 | tf_op jit(solution)/shard_map/ppermute | solution.py:211
  26.6 5.5 %collective-permute-start.5 = (f32[64,128]{1,0:T(8,128)S(1)}, f32[64,128]{1,0:T(8,128)S(1)}, u32[]{:S(2)}, u32[]{:S(2)}) collective-permute-start(f32[64,128]{1,0:T(8,128)S(1)} %shard_map.81.refs_0_), channel_id=1, source_target_pairs={{0,2},{1,3},{2,0},{3,1},{4,6},{5,7},{6,4},{7,5},{8,10},{9,11},{10,... | collective-permute-start | bytes 98312 | tf_op jit(solution)/shard_map/ppermute | solution.py:211
  32.2 4.0 %collective-permute-start.6 = (f32[64,128]{1,0:T(8,128)S(1)}, f32[64,128]{1,0:T(8,128)S(1)}, u32[]{:S(2)}, u32[]{:S(2)}) collective-permute-start(f32[64,128]{1,0:T(8,128)S(1)} %shard_map.84.refs_0_), channel_id=1, source_target_pairs={{0,4},{1,5},{2,6},{3,7},{4,0},{5,1},{6,2},{7,3},{8,12},{9,13},{10,... | collective-permute-start | bytes 98312 | tf_op jit(solution)/shard_map/ppermute | solution.py:211
  36.1 7.8 %collective-permute-start.7 = (f32[64,128]{1,0:T(8,128)S(1)}, f32[64,128]{1,0:T(8,128)S(1)}, u32[]{:S(2)}, u32[]{:S(2)}) collective-permute-start(f32[64,128]{1,0:T(8,128)S(1)} %shard_map.86.refs_0_), channel_id=1, source_target_pairs={{0,8},{1,9},{2,10},{3,11},{4,12},{5,13},{6,14},{7,15},{8,0},{9,1},... | collective-permute-start | bytes 98312 | tf_op jit(solution)/shard_map/ppermute | solution.py:211
  44.0 2.4 %collective-permute-start.8 = (f32[64,128]{1,0:T(8,128)S(1)}, f32[64,128]{1,0:T(8,128)S(1)}, u32[]{:S(2)}, u32[]{:S(2)}) collective-permute-start(f32[64,128]{1,0:T(8,128)S(1)} %shard_map.88.s_ref), channel_id=1, source_target_pairs={{0,1},{1,0},{2,3},{3,2},{4,5},{5,4},{6,7},{7,6},{8,9},{9,8},{10,11... | collective-permute-start | bytes 98312 | tf_op jit(solution)/shard_map/ppermute | solution.py:211
  44.1 2.4 %copy-start = (bf16[8,64,1792]{2,1,0:T(8,128)(2,1)S(1)}, bf16[8,64,1792]{2,1,0:T(8,128)(2,1)}, u32[]{:S(2)}) copy-start(bf16[8,64,1792]{2,1,0:T(8,128)(2,1)} %param.12) | copy-start | bytes 5505028
  44.1 2.4 %copy-start.1 = (bf16[8,64,1792]{2,1,0:T(8,128)(2,1)S(1)}, bf16[8,64,1792]{2,1,0:T(8,128)(2,1)}, u32[]{:S(2)}) copy-start(bf16[8,64,1792]{2,1,0:T(8,128)(2,1)} %param.13) | copy-start | bytes 5505028

commit v3 on v2

--- a/solution.py
+++ b/solution.py
@@ -17,11 +17,17 @@
 VM = pl.BlockSpec(memory_space=pltpu.VMEM)
 HB = pl.BlockSpec(memory_space=pltpu.HBM)
 
-LANE_BITS = ((4, 2, 1), (1, 4, 2))
-SUM_BITS = (1, 2, 4)
+LANE_BITS = ((1, 4, 2), (4, 2, 1))
+SUM_BITS = (4, 2, 1)
 UNIT = 1024
-EARLY = (1, 4, 5)
-LATE = (2, 2, 2, 0)
+COST = 1000
+CUTS = 2
+EARLY = (2, 4, 5)
+TURNS = (4, 4, 4, 2, 2)
+MID = 0
+LATE = (2, 2, 1, 0)
+MAPS = 2
+ROOM = (1, 2, 3)
 
 
 def dot(a, b):
@@ -41,7 +47,7 @@
     return jax.ShapeDtypeStruct(shape, dtype)
 
 
-def call(body, outs, ins, specs=None, scratch=(), vmem=2, bytes_=0, flops=0, alias=None):
+def call(body, outs, ins, specs=None, scratch=(), vmem=None, bytes_=0, flops=0, alias=None):
     return pl.pallas_call(
         body,
         out_shape=outs,
@@ -49,7 +55,7 @@
         out_specs=jax.tree.map(lambda _: VM, outs),
         scratch_shapes=list(scratch),
         input_output_aliases=alias or {},
-        compiler_params=pltpu.CompilerParams(vmem_limit_bytes=int(vmem * MiB)),
+        compiler_params=pltpu.CompilerParams(vmem_limit_bytes=int((vmem or ROOM[0]) * MiB)),
         cost_estimate=pl.CostEstimate(flops=int(flops), bytes_accessed=int(bytes_), transcendentals=0),
     )(*ins)
 
@@ -112,34 +118,48 @@
     refs[-1][...] = total
 
 
-def finish(tg_ref, tu_ref, s_ref, r_ref, v_ref, ag_ref, au_ref, o_ref):
-    _, core = place()
-    mine, other = s_ref[...], r_ref[...]
-    shrink = jnp.concatenate([jnp.where(core == 0, mine, other), jnp.where(core == 0, other, mine)], axis=0)
-    turned = pltpu.roll(shrink, ADAPTER_RANK, 1)
-    column = lax.broadcasted_iota(jnp.int32, shrink.shape, 1)
-    low = column < ADAPTER_RANK
-    version = v_ref[...]
-    half = (column >= ADAPTER_RANK).astype(jnp.int32)
-    wide = []
-    for twice in (jnp.where(low, shrink, turned), jnp.where(low, turned, shrink)):
-        parts = [jnp.where(version == 2 * k + half, twice, 0.0).astype(BF16) for k in range(POLICY_VERSIONS // 2)]
-        wide.append(jnp.concatenate(parts, axis=1))
-    groups = shrink.shape[0] // ROWS_DEV
-    where = {}
-    for core_ in range(2):
-        for spot in range(groups // 2):
-            where[2 * chip_of(core_, spot) + core_] = (core_ * (groups // 2) + spot) * ROWS_DEV
-    for n in range(0, o_ref.shape[1], 256):
-        gate = tg_ref[:, n : n + 256] + adapter_scale * dot(wide[0], ag_ref[:, n : n + 256])
-        up = tu_ref[:, n : n + 256] + adapter_scale * dot(wide[1], au_ref[:, n : n + 256])
-        hidden = gate / (1.0 + jnp.exp(-gate)) * up
-        for r in range(0, groups, 2):
-            two = [hidden[where[k] : where[k] + ROWS_DEV] for k in (r, r + 1)]
-            o_ref[r * ROWS_DEV : (r + 2) * ROWS_DEV, n : n + 256] = jnp.concatenate(two, axis=0).astype(BF16)
-
-
-def work(todo, x, have, units, hbm, totals):
+def finish(todo, x, have, totals, part, got, version, ag, au):
+    rows, cols = totals[0].shape
+    nt = len(todo)
+
+    def body(x_ref, *refs):
+        w_refs, (tg_ref, tu_ref, s_ref, r_ref, v_ref, ag_ref, au_ref, o_ref) = refs[:nt], refs[nt:]
+        _, core = place()
+        mine, other = s_ref[...], r_ref[...]
+        shrink = jnp.concatenate([jnp.where(core == 0, mine, other), jnp.where(core == 0, other, mine)], axis=0)
+        turned = pltpu.roll(shrink, ADAPTER_RANK, 1)
+        column = lax.broadcasted_iota(jnp.int32, shrink.shape, 1)
+        low = column < ADAPTER_RANK
+        version = v_ref[...]
+        half = (column >= ADAPTER_RANK).astype(jnp.int32)
+        wide = []
+        for twice in (jnp.where(low, shrink, turned), jnp.where(low, turned, shrink)):
+            parts = [jnp.where(version == 2 * k + half, twice, 0.0).astype(BF16) for k in range(POLICY_VERSIONS // 2)]
+            wide.append(jnp.concatenate(parts, axis=1))
+        groups = rows // ROWS_DEV
+        where = {}
+        for core_ in range(2):
+            for spot in range(groups // 2):
+                where[2 * chip_of(core_, spot) + core_] = (core_ * (groups // 2) + spot) * ROWS_DEV
+        for n in range(0, cols, 256):
+            both = []
+            for m, (t_ref, a_ref) in enumerate(((tg_ref, ag_ref), (tu_ref, au_ref))):
+                total = t_ref[:, n : n + 256]
+                for (m2, k), w_ref in zip(todo, w_refs):
+                    if m2 == m:
+                        total = total + dot(x_ref[:, k * UNIT : (k + 1) * UNIT], w_ref[:, n : n + 256])
+                both.append(total + adapter_scale * dot(wide[m], a_ref[:, n : n + 256]))
+            gate, up = both
+            hidden = gate / (1.0 + jnp.exp(-gate)) * up
+            for r in range(0, groups, 2):
+                two = [hidden[where[k] : where[k] + ROWS_DEV] for k in (r, r + 1)]
+                o_ref[r * ROWS_DEV : (r + 2) * ROWS_DEV, n : n + 256] = jnp.concatenate(two, axis=0).astype(BF16)
+
+    ins = (x, *[have[t] for t in todo], *totals, part, got, version, ag, au)
+    return call(body, like((rows, cols)), ins, vmem=ROOM[2])
+
+
+def work(todo, x, have, units, hbm, totals, counts=None, maps=(), after=None):
     cols = hbm[0].shape[1]
     done = sorted({m for m, _ in todo})
     old = [m for m in done if totals[m] is not None]
@@ -152,17 +172,29 @@
             got, refs[:] = refs[:n], refs[n:]
             return got
 
+        take(1 if after is not None else 0)
+        c_refs, map_refs = take(1 if counts is not None else 0), take(len(maps))
         x_refs, w_refs, hbm_refs = take(1 if nt else 0), take(nt), take(2)
         old_refs, new_refs = dict(zip(old, take(len(old)))), dict(zip(done, take(len(done))))
+        to_refs, v_refs, got_refs = take(nu), take(len(c_refs)), take(len(maps))
+        if c_refs:
+            small = pltpu.make_async_copy(c_refs[0], refs[1], refs[2])
+            small.start()
         copies = [
             pltpu.make_async_copy(
-                hbm_refs[m].at[pl.ds(k * UNIT + h * UNIT // 2, UNIT // 2), :], to_ref.at[pl.ds(h * UNIT // 2, UNIT // 2), :], refs[nu].at[2 * i + h]
+                hbm_refs[m].at[pl.ds(k * UNIT + h * UNIT // CUTS, UNIT // CUTS), :],
+                to_ref.at[pl.ds(h * UNIT // CUTS, UNIT // CUTS), :],
+                refs[0].at[CUTS * i + h],
             )
-            for i, ((m, k), to_ref) in enumerate(zip(units, refs[:nu]))
-            for h in range(2)
+            for i, ((m, k), to_ref) in enumerate(zip(units, to_refs))
+            for h in range(CUTS)
         ]
+        copies += [pltpu.make_async_copy(f, t, refs[0].at[CUTS * nu + i]) for i, (f, t) in enumerate(zip(map_refs, got_refs))]
         for c in copies:
             c.start()
+        if c_refs:
+            small.wait()
+            versions(refs[1], v_refs[0])
 
         @pl.when(lax.axis_index("rep") >= 0)
         def _():
@@ -180,19 +212,31 @@
 
     ins = ([x] if nt else []) + [have[t] for t in todo]
     specs = [VM] * len(ins) + [HB] * 2 + [VM] * len(old)
+    ncopy = CUTS * nu + len(maps)
+    scratch = [pltpu.SemaphoreType.DMA((ncopy,))] if ncopy else []
+    ins, specs = [*maps, *ins], [HB] * len(maps) + specs
+    if counts is not None:
+        ins, specs = [counts, *ins], [HB, *specs]
+        scratch += [pltpu.VMEM(counts.shape, counts.dtype), pltpu.SemaphoreType.DMA]
+    if after is not None:
+        ins, specs = [after, *ins], [VM, *specs]
     ins += hbm
     alias = {len(ins) + i: done.index(m) for i, m in enumerate(old)}
     ins += [totals[m] for m in old]
     rows = x.shape[0] if nt else 0
     outs = [like((rows, cols), F32) for _ in done] + [like((UNIT, cols)) for _ in units]
+    if counts is not None:
+        outs.append(like((counts.shape[1] * ROWS_DEV, 128), jnp.int32))
+    outs += [like(f.shape) for f in maps]
     got = call(
-        body, outs, ins, specs, [pltpu.SemaphoreType.DMA((2 * nu,))] if nu else [], vmem=4, alias=alias,
-        bytes_=UNIT * cols * 2 * max(nt, nu), flops=2 * rows * UNIT * cols * nt,
+        body, outs, ins, specs, scratch, vmem=ROOM[1], alias=alias,
+        bytes_=COST,
     )
     for m, t in zip(done, got):
         totals[m] = t
     for unit, w in zip(units, got[len(done) :]):
         have[unit] = pltpu.with_memory_space_constraint(w, pltpu.VMEM)
+    return got[len(done) + nu :]
 
 
 def cores():
@@ -225,36 +269,42 @@
     rows = counts.shape[0] * ROWS_DEV
     order = [(m, k) for k in range(feats // UNIT) for m in range(2)]
     early = split(order, EARLY)
-    late = split(order[sum(EARLY) :], LATE)
+    late = split(order[sum(EARLY) + MID :], LATE)
     have, totals = {}, [None, None]
     a = x
     for step in range(3):
         r = permute(a, lanes(step))
         if step == 0:
             e = permute(down, cores())
-            version = call(versions, like((rows, 128), jnp.int32), (counts.T,))
-        work([], None, have, early[step], hbm, totals)
+            (version,) = work([], None, have, early[step], hbm, totals, pltpu.with_memory_space_constraint(counts.T, pltpu.HBM))
+        else:
+            work([], None, have, early[step], hbm, totals)
         last = early[step][-1]
         if step == 0:
-            r, version, have[last] = hold(r, version, have[last])
+            r, e, version, have[last] = hold(r, e, version, have[last])
         else:
             r, have[last] = hold(r, have[last])
         a = call(functools.partial(double, step), like((a.shape[0] * 2, feats)), (a, r))
     other = permute(a, cores())
     part = call(partial, like((rows // 2, 128), F32), (a, down, e, version))
     got = permute(part, chips(SUM_BITS[0]))
+    if MID:
+        last = order[sum(EARLY) + MID - 1]
+        work([], None, have, order[sum(EARLY) :][:MID], hbm, totals, after=part)
+        other, have[last] = hold(other, have[last])
     x = call(join, like((rows, feats)), (a, other))
-    per = len(order) // 4
+    turns = split(order, TURNS)
+    wide = POLICY_VERSIONS * ADAPTER_RANK
+    maps = [pltpu.with_memory_space_constraint(w.reshape(wide, cols), pltpu.HBM) for w in (ag, au)]
     for j in range(4):
-        work(order[per * j : per * (j + 1)], x, have, late[j], hbm, totals)
+        fetched = work(turns[j], x, have, late[j], hbm, totals, maps=maps if j == MAPS else ())
+        if j == MAPS:
+            maps = [pltpu.with_memory_space_constraint(w, pltpu.VMEM) for w in fetched]
         if j < 3:
             got, totals[0] = hold(got, totals[0])
             part = call(add, like((rows // 2, 128), F32), (part, got))
             got = permute(part, chips(SUM_BITS[j + 1]) if j < 2 else cores())
-    wide = POLICY_VERSIONS * ADAPTER_RANK
-    return call(
-        finish, like((rows, cols)), (*totals, part, got, version, ag.reshape(wide, cols), au.reshape(wide, cols)), vmem=6
-    )
+    return finish(turns[4], x, have, totals, part, got, version, *maps)
 
 
 def row_versions(counts):

time: 48.1 us -> 46.5 us (0.967)
  starting transfers between devices: 16.4 us -> 15.3 us
  Pallas kernels: 28.4 us -> 29.1 us
  local copies, waits for them, and re-layouts: 0.71 us -> 0.01 us
  waiting for transfers between devices: 2.26 us -> 1.76 us
    ppermute x9, starting transfers between devices: 16.4 us -> 15.3 us  [permute(): return lax.ppermute(x, 'rep', pairs)]
    unnamed x10 -> x4, local copies, waits for them, and re-layouts: 0.71 us -> 0.01 us
    pallas_call x17 -> x16, Pallas kernels: 28.4 us -> 29.1 us  [call(): pl.pallas_call(body, out_shape=outs, in_specs=[VM] * len(ins) if specs is...]
    ppermute x9, waiting for transfers between devices: 2.26 us -> 1.76 us  [permute(): return lax.ppermute(x, 'rep', pairs)]
  transfers between devices with their start and end apart: 9 -> 9, of which waited for: 4 -> 2; matrix products, arithmetic and copies ran while one was open for 0% -> 0% of each run, Pallas kernels for 56% -> 57%
where the time goes in v3:
time: 46.5 us; the launch traced here: 46.3 us
  Pallas kernels  29.1 us (63%)
  starting transfers between devices  15.3 us (33%)
  waiting for transfers between devices  1.76 us (4%)
    pallas_call x16, Pallas kernels, call(): pl.pallas_call(body, out_shape=outs, in_specs=[VM] * len(ins) if specs is...  29.1 us
    ppermute x9, starting transfers between devices, permute(): return lax.ppermute(x, 'rep', pairs)  15.3 us
    ppermute x9, waiting for transfers between devices, permute(): return lax.ppermute(x, 'rep', pairs)  1.76 us
  transfers between devices with their start and end apart: 9, of which 2 were waited for; matrix products, arithmetic and copies ran while one was open for 0% of the time, Pallas kernels for 57%

profile of v3, /device:TPU:0, one launch (start us, length us, event | category | flops | bytes accessed | tf_op | source)
XLA Modules:
  0.0 46.3 jit_solution(2109512143701000954)
XLA Ops:
  0.0 0.5 collective-permute-start.1
  0.5 2.5 %collective-permute-start = (bf16[8,8192]{1,0:T(8,128)(2,1)}, bf16[8,8192]{1,0:T(8,128)(2,1)S(1)}, u32[]{:S(2)}, u32[]{:S(2)}) collective-permute-start(bf16[8,8192]{1,0:T(8,128)(2,1)} %m_ref.1), channel_id=1, source_target_pairs={{0,2},{1,9},{2,0},{3,11},{4,6},{5,13},{6,4},{7,15},{8,10},{9,1},{1... | collective-permute-start | bytes 393224 | tf_op jit(solution)/shard_map/ppermute | solution.py:255
  3.0 0.0 copy-start.1
  3.0 3.2 %shard_map.73 = (bf16[1024,1792]{1,0:T(8,128)(2,1)S(1)}, bf16[1024,1792]{1,0:T(8,128)(2,1)S(1)}, s32[128,128]{1,0:T(8,128)S(1)}) custom-call(s32[8,16]{1,0:T(8,128)} %bitcast.5, bf16[8192,1792]{1,0:T(8,128)(2,1)} %refs_3_.1, bf16[8192,1792]{1,0:T(8,128)(2,1)} %refs_4_.1), custom_call_target="tpu_custom_call" | custom-call | bytes 1000 | tf_op jit(solution)/shard_map/pallas_call | solution.py:51
  6.2 0.0 collective-permute-done.r_ref
  6.2 0.0 collective-permute-done.1.e_ref
  6.2 0.0 copy-done.1
  6.2 0.1 shard_map.74.m_ref
  6.3 3.0 %collective-permute-start.2 = (bf16[16,8192]{1,0:T(8,128)(2,1)S(1)}, bf16[16,8192]{1,0:T(8,128)(2,1)S(1)}, u32[]{:S(2)}, u32[]{:S(2)}) collective-permute-start(bf16[16,8192]{1,0:T(8,128)(2,1)S(1)} %shard_map.74.m_ref), channel_id=1, source_target_pairs={{0,8},{1,5},{2,10},{3,7},{4,12},{5,1},{6,14},{7,3},{8,0},{9,13},{1... | collective-permute-start | bytes 786440 | tf_op jit(solution)/shard_map/ppermute | solution.py:255
  9.4 5.3 %shard_map.75 = (bf16[1024,1792]{1,0:T(8,128)(2,1)S(1)}, bf16[1024,1792]{1,0:T(8,128)(2,1)S(1)}, bf16[1024,1792]{1,0:T(8,128)(2,1)S(1)}, bf16[1024,1792]{1,0:T(8,128)(2,1)S(1)}) custom-call(bf16[8192,1792]{1,0:T(8,128)(2,1)} %refs_3_.1, bf16[8192,1792]{1,0:T(8,128)(2,1)} %refs_4_.1), custom_call_target="tpu_custom_call" | custom-call | bytes 1000 | tf_op jit(solution)/shard_map/pallas_call | solution.py:51
  14.7 1.0 %collective-permute-done.2.r_ref = bf16[16,8192]{1,0:T(8,128)(2,1)S(1)} collective-permute-done((bf16[16,8192]{1,0:T(8,128)(2,1)S(1)}, bf16[16,8192]{1,0:T(8,128)(2,1)S(1)}, u32[]{:S(2)}, u32[]{:S(2)}) %collective-permute-start.2) | collective-permute-done | bytes 262176 | tf_op jit(solution)/shard_map/ppermute | solution.py:255
  15.6 0.1 shard_map.76.m_ref
  15.7 0.0 copy-start
  15.7 2.4 %collective-permute-start.3 = (bf16[32,8192]{1,0:T(8,128)(2,1)S(1)}, bf16[32,8192]{1,0:T(8,128)(2,1)S(1)}, u32[]{:S(2)}, u32[]{:S(2)}) collective-permute-start(bf16[32,8192]{1,0:T(8,128)(2,1)S(1)} %shard_map.76.m_ref), channel_id=1, source_target_pairs={{0,4},{1,3},{2,6},{3,1},{4,0},{5,7},{6,2},{7,5},{8,12},{9,11},{10,... | collective-permute-start | bytes 1572872 | tf_op jit(solution)/shard_map/ppermute | solution.py:255
  18.1 6.4 %shard_map.77 = (bf16[1024,1792]{1,0:T(8,128)(2,1)S(1)}, bf16[1024,1792]{1,0:T(8,128)(2,1)S(1)}, bf16[1024,1792]{1,0:T(8,128)(2,1)S(1)}, bf16[1024,1792]{1,0:T(8,128)(2,1)S(1)}, bf16[1024,1792]{1,0:T(8,128)(2,1)S(1)}) custom-call(bf16[8192,1792]{1,0:T(8,128)(2,1)} %refs_3_.1, bf16[8192,1792]{1,0:T(8,128)(2,1)} %refs_4_.1), custom_call_target="tpu_custom_call" | custom-call | bytes 1000 | tf_op jit(solution)/shard_map/pallas_call | solution.py:51
  24.5 0.8 %collective-permute-done.3.r_ref = bf16[32,8192]{1,0:T(8,128)(2,1)S(1)} collective-permute-done((bf16[32,8192]{1,0:T(8,128)(2,1)S(1)}, bf16[32,8192]{1,0:T(8,128)(2,1)S(1)}, u32[]{:S(2)}, u32[]{:S(2)}) %collective-permute-start.3) | collective-permute-done | bytes 524320 | tf_op jit(solution)/shard_map/ppermute | solution.py:255
  25.3 0.1 shard_map.78.m_ref.x_ref
  25.4 0.1 collective-permute-start.4
  25.5 0.0 copy-done
  25.5 0.4 shard_map.80.refs_0_
  25.9 3.0 %collective-permute-start.5 = (f32[64,128]{1,0:T(8,128)S(1)}, f32[64,128]{1,0:T(8,128)S(1)}, u32[]{:S(2)}, u32[]{:S(2)}) collective-permute-start(f32[64,128]{1,0:T(8,128)S(1)} %shard_map.80.refs_0_), channel_id=1, source_target_pairs={{0,8},{1,9},{2,10},{3,11},{4,12},{5,13},{6,14},{7,15},{8,0},{9,1},... | collective-permute-start | bytes 98312 | tf_op jit(solution)/shard_map/ppermute | solution.py:255
  29.0 0.0 collective-permute-done.4.r_ref
  29.0 0.1 shard_map.79.refs_0_.refs_2_.x_ref
  29.1 3.2 %shard_map.81 = (f32[128,1792]{1,0:T(8,128)S(1)}, f32[128,1792]{1,0:T(8,128)S(1)}, bf16[1024,1792]{1,0:T(8,128)(2,1)S(1)}, bf16[1024,1792]{1,0:T(8,128)(2,1)S(1)}) custom-call(bf16[128,8192]{1,0:T(8,128)(2,1)S(1)} %shard_map.79.refs_0_.refs_2_.x_ref, bf16[1024,1792]{1,0:T(8,128)(2,1)S(1)} %get-tuple-element.59.refs_1_, ...), custom_call_target="tpu_custom_call" | custom-call | bytes 1000 | tf_op jit(solution)/shard_map/pallas_call | solution.py:51
  32.3 0.0 collective-permute-done.5.refs_1_
  32.3 2.1 %collective-permute-start.6 = (f32[64,128]{1,0:T(8,128)S(1)}, f32[64,128]{1,0:T(8,128)S(1)}, u32[]{:S(2)}, u32[]{:S(2)}) collective-permute-start(f32[64,128]{1,0:T(8,128)S(1)} %shard_map.83.refs_0_), channel_id=1, source_target_pairs={{0,4},{1,5},{2,6},{3,7},{4,0},{5,1},{6,2},{7,3},{8,12},{9,13},{10,... | collective-permute-start | bytes 98312 | tf_op jit(solution)/shard_map/ppermute | solution.py:255
  34.4 3.2 %shard_map.82 = (f32[128,1792]{1,0:T(8,128)S(1)}, f32[128,1792]{1,0:T(8,128)S(1)}, bf16[1024,1792]{1,0:T(8,128)(2,1)S(1)}, bf16[1024,1792]{1,0:T(8,128)(2,1)S(1)}) custom-call(bf16[128,8192]{1,0:T(8,128)(2,1)S(1)} %shard_map.79.refs_0_.refs_2_.x_ref, bf16[1024,1792]{1,0:T(8,128)(2,1)S(1)} %get-tuple-element.53.refs_1_, ...), custom_call_target="tpu_custom_call", output_to_operand_aliasing={{0}: (7, {}), {1}: (8, {})} | custom-call | bytes 1000 | tf_op jit(solution)/shard_map/pallas_call | solution.py:51
  37.6 0.0 collective-permute-done.6.refs_1_
  37.6 1.6 %collective-permute-start.7 = (f32[64,128]{1,0:T(8,128)S(1)}, f32[64,128]{1,0:T(8,128)S(1)}, u32[]{:S(2)}, u32[]{:S(2)}) collective-permute-start(f32[64,128]{1,0:T(8,128)S(1)} %shard_map.85.refs_0_), channel_id=1, source_target_pairs={{0,2},{1,3},{2,0},{3,1},{4,6},{5,7},{6,4},{7,5},{8,10},{9,11},{10,... | collective-permute-start | bytes 98312 | tf_op jit(solution)/shard_map/ppermute | solution.py:255
  39.2 3.2 %shard_map.84 = (f32[128,1792]{1,0:T(8,128)S(1)}, f32[128,1792]{1,0:T(8,128)S(1)}, bf16[1024,1792]{1,0:T(8,128)(2,1)S(1)}, bf16[512,1792]{1,0:T(8,128)(2,1)S(1)}, bf16[512,1792]{1,0:T(8,128)(2,1)S(1)}) custom-call(bf16[512,1792]{1,0:T(8,128)(2,1)} %bitcast.3, bf16[512,1792]{1,0:T(8,128)(2,1)} %bitcast.4, ...), custom_call_target="tpu_custom_call", output_to_operand_aliasing={{0}: (9, {}), {1}: (10, {})} | custom-call | bytes 1000 | tf_op jit(solution)/shard_map/pallas_call | solution.py:51
  42.4 0.0 collective-permute-done.7.refs_1_
  42.5 0.1 collective-permute-start.8
  42.5 1.3 %shard_map.86 = (f32[128,1792]{1,0:T(8,128)S(1)}, f32[128,1792]{1,0:T(8,128)S(1)}) custom-call(bf16[128,8192]{1,0:T(8,128)(2,1)S(1)} %shard_map.79.refs_0_.refs_2_.x_ref, bf16[1024,1792]{1,0:T(8,128)(2,1)S(1)} %get-tuple-element.76.refs_1_, bf16[1024,1792]{1,0:T(8,128)(2,1)S(1)} %get-tuple-element.77.refs_2_, ...), custom_call_target="tpu_custom_call", output_to_operand_aliasing={{0}: (5, {}), {1}: (6, {})} | custom-call | bytes 1000 | tf_op jit(solution)/shard_map/pallas_call | solution.py:51
  43.9 0.0 collective-permute-done.8.refs_5_
  43.9 2.4 %shard_map.88 = bf16[128,1792]{1,0:T(8,128)(2,1)} custom-call(bf16[128,8192]{1,0:T(8,128)(2,1)S(1)} %shard_map.79.refs_0_.refs_2_.x_ref, bf16[1024,1792]{1,0:T(8,128)(2,1)S(1)} %get-tuple-element.66.refs_0_, bf16[1024,1792]{1,0:T(8,128)(2,1)S(1)} %get-tuple-element.75.refs_1_, f32[128,1792]{1,0:T(8,128)S(1)} %get-tuple-element.82.refs_2_, ...), custom_call_target="tpu_custom_call" | custom-call | tf_op jit(solution)/shard_map/pallas_call | solution.py:51
  (3 shorter events, 0.0 us)
Async XLA Ops:
  0.0 6.2 %collective-permute-start.1 = (bf16[8,512,128]{2,1,0:T(8,128)(2,1)}, bf16[8,512,128]{2,1,0:T(8,128)(2,1)S(1)}, u32[]{:S(2)}, u32[]{:S(2)}) collective-permute-start(bf16[8,512,128]{2,1,0:T(8,128)(2,1)} %d_ref.1), channel_id=1, source_target_pairs={{0,1},{1,0},{2,3},{3,2},{4,5},{5,4},{6,7},{7,6},{8,9},{9,8},{10,11... | collective-permute-start | bytes 3145736 | tf_op jit(solution)/shard_map/ppermute | solution.py:255
  0.5 5.8 %collective-permute-start = (bf16[8,8192]{1,0:T(8,128)(2,1)}, bf16[8,8192]{1,0:T(8,128)(2,1)S(1)}, u32[]{:S(2)}, u32[]{:S(2)}) collective-permute-start(bf16[8,8192]{1,0:T(8,128)(2,1)} %m_ref.1), channel_id=1, source_target_pairs={{0,2},{1,9},{2,0},{3,11},{4,6},{5,13},{6,4},{7,15},{8,10},{9,1},{1... | collective-permute-start | bytes 393224 | tf_op jit(solution)/shard_map/ppermute | solution.py:255
  3.0 3.3 %copy-start.1 = (bf16[8,8192]{1,0:T(8,128)(2,1)S(1)}, bf16[8,8192]{1,0:T(8,128)(2,1)}, u32[]{:S(2)}) copy-start(bf16[8,8192]{1,0:T(8,128)(2,1)} %m_ref.1) | copy-start | bytes 393220
  6.3 9.3 %collective-permute-start.2 = (bf16[16,8192]{1,0:T(8,128)(2,1)S(1)}, bf16[16,8192]{1,0:T(8,128)(2,1)S(1)}, u32[]{:S(2)}, u32[]{:S(2)}) collective-permute-start(bf16[16,8192]{1,0:T(8,128)(2,1)S(1)} %shard_map.74.m_ref), channel_id=1, source_target_pairs={{0,8},{1,5},{2,10},{3,7},{4,12},{5,1},{6,14},{7,3},{8,0},{9,13},{1... | collective-permute-start | bytes 786440 | tf_op jit(solution)/shard_map/ppermute | solution.py:255
  15.7 9.8 %copy-start = (bf16[8,512,128]{2,1,0:T(8,128)(2,1)S(1)}, bf16[8,512,128]{2,1,0:T(8,128)(2,1)}, u32[]{:S(2)}) copy-start(bf16[8,512,128]{2,1,0:T(8,128)(2,1)} %d_ref.1) | copy-start | bytes 3145732
  15.7 9.5 %collective-permute-start.3 = (bf16[32,8192]{1,0:T(8,128)(2,1)S(1)}, bf16[32,8192]{1,0:T(8,128)(2,1)S(1)}, u32[]{:S(2)}, u32[]{:S(2)}) collective-permute-start(bf16[32,8192]{1,0:T(8,128)(2,1)S(1)} %shard_map.76.m_ref), channel_id=1, source_target_pairs={{0,4},{1,3},{2,6},{3,1},{4,0},{5,7},{6,2},{7,5},{8,12},{9,11},{10,... | collective-permute-start | bytes 1572872 | tf_op jit(solution)/shard_map/ppermute | solution.py:255
  25.4 3.6 %collective-permute-start.4 = (bf16[64,8192]{1,0:T(8,128)(2,1)S(1)}, bf16[64,8192]{1,0:T(8,128)(2,1)S(1)}, u32[]{:S(2)}, u32[]{:S(2)}) collective-permute-start(bf16[64,8192]{1,0:T(8,128)(2,1)S(1)} %shard_map.78.m_ref.x_ref), channel_id=1, source_target_pairs={{0,1},{1,0},{2,3},{3,2},{4,5},{5,4},{6,7},{7,6},{8,9},{9,8},{10,11... | collective-permute-start | bytes 3145736 | tf_op jit(solution)/shard_map/ppermute | solution.py:255
  25.9 6.4 %collective-permute-start.5 = (f32[64,128]{1,0:T(8,128)S(1)}, f32[64,128]{1,0:T(8,128)S(1)}, u32[]{:S(2)}, u32[]{:S(2)}) collective-permute-start(f32[64,128]{1,0:T(8,128)S(1)} %shard_map.80.refs_0_), channel_id=1, source_target_pairs={{0,8},{1,9},{2,10},{3,11},{4,12},{5,13},{6,14},{7,15},{8,0},{9,1},... | collective-permute-start | bytes 98312 | tf_op jit(solution)/shard_map/ppermute | solution.py:255
  32.3 5.3 %collective-permute-start.6 = (f32[64,128]{1,0:T(8,128)S(1)}, f32[64,128]{1,0:T(8,128)S(1)}, u32[]{:S(2)}, u32[]{:S(2)}) collective-permute-start(f32[64,128]{1,0:T(8,128)S(1)} %shard_map.83.refs_0_), channel_id=1, source_target_pairs={{0,4},{1,5},{2,6},{3,7},{4,0},{5,1},{6,2},{7,3},{8,12},{9,13},{10,... | collective-permute-start | bytes 98312 | tf_op jit(solution)/shard_map/ppermute | solution.py:255
  37.6 4.8 %collective-permute-start.7 = (f32[64,128]{1,0:T(8,128)S(1)}, f32[64,128]{1,0:T(8,128)S(1)}, u32[]{:S(2)}, u32[]{:S(2)}) collective-permute-start(f32[64,128]{1,0:T(8,128)S(1)} %shard_map.85.refs_0_), channel_id=1, source_target_pairs={{0,2},{1,3},{2,0},{3,1},{4,6},{5,7},{6,4},{7,5},{8,10},{9,11},{10,... | collective-permute-start | bytes 98312 | tf_op jit(solution)/shard_map/ppermute | solution.py:255
  42.5 1.4 %collective-permute-start.8 = (f32[64,128]{1,0:T(8,128)S(1)}, f32[64,128]{1,0:T(8,128)S(1)}, u32[]{:S(2)}, u32[]{:S(2)}) collective-permute-start(f32[64,128]{1,0:T(8,128)S(1)} %shard_map.87.refs_4_), channel_id=1, source_target_pairs={{0,1},{1,0},{2,3},{3,2},{4,5},{5,4},{6,7},{7,6},{8,9},{9,8},{10,11... | collective-permute-start | bytes 98312 | tf_op jit(solution)/shard_map/ppermute | solution.py:255

commit v4 on v3

--- a/solution.py
+++ b/solution.py
@@ -21,12 +21,12 @@
 SUM_BITS = (4, 2, 1)
 UNIT = 1024
 COST = 1000
-CUTS = 2
+CUTS = 1
 EARLY = (2, 4, 5)
 TURNS = (4, 4, 4, 2, 2)
 MID = 0
-LATE = (2, 2, 1, 0)
-MAPS = 2
+LATE = (1, 2, 2, 0)
+MAPS = 3
 ROOM = (1, 2, 3)
 
 
@@ -74,11 +74,14 @@
         o_ref[pl.ds(pl.multiple_of((1 - bit) * rows, rows), rows), :] = r_ref[...]
 
 
-def join(m_ref, r_ref, o_ref):
-    _, core = place()
-    rows = m_ref.shape[0]
+def join(m_ref, a_ref, r_ref, o_ref):
+    chip, core = place()
+    rows, part = m_ref.shape[0], a_ref.shape[0]
     o_ref[pl.ds(pl.multiple_of(core * rows, rows), rows), :] = m_ref[...]
-    o_ref[pl.ds(pl.multiple_of((1 - core) * rows, rows), rows), :] = r_ref[...]
+    bit = jnp.where(core == 0, lax.rem(chip // LANE_BITS[1][2], 2), lax.rem(chip // LANE_BITS[0][2], 2))
+    base = (1 - core) * rows
+    o_ref[pl.ds(pl.multiple_of(base + bit * part, part), part), :] = a_ref[...]
+    o_ref[pl.ds(pl.multiple_of(base + (1 - bit) * part, part), part), :] = r_ref[...]
 
 
 def versions(c_ref, o_ref):
@@ -274,6 +277,8 @@
     a = x
     for step in range(3):
         r = permute(a, lanes(step))
+        if step == 2:
+            held = permute(a, cores())
         if step == 0:
             e = permute(down, cores())
             (version,) = work([], None, have, early[step], hbm, totals, pltpu.with_memory_space_constraint(counts.T, pltpu.HBM))
@@ -284,15 +289,17 @@
             r, e, version, have[last] = hold(r, e, version, have[last])
         else:
             r, have[last] = hold(r, have[last])
+        if step == 2:
+            held, r = hold(held, r)
+            other = permute(r, cores())
         a = call(functools.partial(double, step), like((a.shape[0] * 2, feats)), (a, r))
-    other = permute(a, cores())
     part = call(partial, like((rows // 2, 128), F32), (a, down, e, version))
     got = permute(part, chips(SUM_BITS[0]))
     if MID:
         last = order[sum(EARLY) + MID - 1]
         work([], None, have, order[sum(EARLY) :][:MID], hbm, totals, after=part)
         other, have[last] = hold(other, have[last])
-    x = call(join, like((rows, feats)), (a, other))
+    x = call(join, like((rows, feats)), (a, held, other))
     turns = split(order, TURNS)
     wide = POLICY_VERSIONS * ADAPTER_RANK
     maps = [pltpu.with_memory_space_constraint(w.reshape(wide, cols), pltpu.HBM) for w in (ag, au)]

time: 46.5 us -> 46 us (0.989)
  Pallas kernels: 29.1 us -> 28.6 us
    pallas_call x16, Pallas kernels: 29.1 us -> 28.6 us  [call(): pl.pallas_call(body, out_shape=outs, in_specs=[VM] * len(ins) if specs is...]
    ppermute x9 -> x10, waiting for transfers between devices: 1.76 us -> 1.83 us  [permute(): return lax.ppermute(x, 'rep', pairs)]
    ppermute x9 -> x10, starting transfers between devices: 15.3 us -> 15.2 us  [permute(): return lax.ppermute(x, 'rep', pairs)]
  transfers between devices with their start and end apart: 9 -> 10, of which waited for: 2 -> 2; matrix products, arithmetic and copies ran while one was open for 0% -> 0% of each run, Pallas kernels for 57% -> 57%
where the time goes in v4:
time: 46 us; the launch traced here: 45.9 us
  Pallas kernels  28.6 us (62%)
  starting transfers between devices  15.2 us (33%)
  waiting for transfers between devices  1.83 us (4%)
    pallas_call x16, Pallas kernels, call(): pl.pallas_call(body, out_shape=outs, in_specs=[VM] * len(ins) if specs is...  28.6 us
    ppermute x10, starting transfers between devices, permute(): return lax.ppermute(x, 'rep', pairs)  15.2 us
    ppermute x10, waiting for transfers between devices, permute(): return lax.ppermute(x, 'rep', pairs)  1.83 us
  transfers between devices with their start and end apart: 10, of which 2 were waited for; matrix products, arithmetic and copies ran while one was open for 0% of the time, Pallas kernels for 57%

profile of v4, /device:TPU:0, one launch (start us, length us, event | category | flops | bytes accessed | tf_op | source)
XLA Modules:
  0.0 45.9 jit_solution(9858152093661753587)
XLA Ops:
  0.0 0.5 collective-permute-start.1
  0.5 2.5 %collective-permute-start = (bf16[8,8192]{1,0:T(8,128)(2,1)}, bf16[8,8192]{1,0:T(8,128)(2,1)S(1)}, u32[]{:S(2)}, u32[]{:S(2)}) collective-permute-start(bf16[8,8192]{1,0:T(8,128)(2,1)} %m_ref.1), channel_id=1, source_target_pairs={{0,2},{1,9},{2,0},{3,11},{4,6},{5,13},{6,4},{7,15},{8,10},{9,1},{1... | collective-permute-start | bytes 393224 | tf_op jit(solution)/shard_map/ppermute | solution.py:258
  3.0 0.0 copy-start.1
  3.0 3.2 %shard_map.73 = (bf16[1024,1792]{1,0:T(8,128)(2,1)S(1)}, bf16[1024,1792]{1,0:T(8,128)(2,1)S(1)}, s32[128,128]{1,0:T(8,128)S(1)}) custom-call(s32[8,16]{1,0:T(8,128)} %bitcast.5, bf16[8192,1792]{1,0:T(8,128)(2,1)} %refs_5_.7, bf16[8192,1792]{1,0:T(8,128)(2,1)} %refs_6_.7), custom_call_target="tpu_custom_call" | custom-call | bytes 1000 | tf_op jit(solution)/shard_map/pallas_call | solution.py:51
  6.2 0.0 collective-permute-done.r_ref
  6.2 0.0 collective-permute-done.1.e_ref
  6.2 0.0 copy-done.1
  6.2 0.1 shard_map.74.m_ref
  6.3 3.0 %collective-permute-start.2 = (bf16[16,8192]{1,0:T(8,128)(2,1)S(1)}, bf16[16,8192]{1,0:T(8,128)(2,1)S(1)}, u32[]{:S(2)}, u32[]{:S(2)}) collective-permute-start(bf16[16,8192]{1,0:T(8,128)(2,1)S(1)} %shard_map.74.m_ref), channel_id=1, source_target_pairs={{0,8},{1,5},{2,10},{3,7},{4,12},{5,1},{6,14},{7,3},{8,0},{9,13},{1... | collective-permute-start | bytes 786440 | tf_op jit(solution)/shard_map/ppermute | solution.py:258
  9.4 5.3 %shard_map.75 = (bf16[1024,1792]{1,0:T(8,128)(2,1)S(1)}, bf16[1024,1792]{1,0:T(8,128)(2,1)S(1)}, bf16[1024,1792]{1,0:T(8,128)(2,1)S(1)}, bf16[1024,1792]{1,0:T(8,128)(2,1)S(1)}) custom-call(bf16[8192,1792]{1,0:T(8,128)(2,1)} %refs_5_.7, bf16[8192,1792]{1,0:T(8,128)(2,1)} %refs_6_.7), custom_call_target="tpu_custom_call" | custom-call | bytes 1000 | tf_op jit(solution)/shard_map/pallas_call | solution.py:51
  14.7 1.0 %collective-permute-done.2.r_ref = bf16[16,8192]{1,0:T(8,128)(2,1)S(1)} collective-permute-done((bf16[16,8192]{1,0:T(8,128)(2,1)S(1)}, bf16[16,8192]{1,0:T(8,128)(2,1)S(1)}, u32[]{:S(2)}, u32[]{:S(2)}) %collective-permute-start.2) | collective-permute-done | bytes 262176 | tf_op jit(solution)/shard_map/ppermute | solution.py:258
  15.6 0.1 shard_map.76.m_ref
  15.7 0.0 copy-start
  15.7 2.4 %collective-permute-start.4 = (bf16[32,8192]{1,0:T(8,128)(2,1)S(1)}, bf16[32,8192]{1,0:T(8,128)(2,1)S(1)}, u32[]{:S(2)}, u32[]{:S(2)}) collective-permute-start(bf16[32,8192]{1,0:T(8,128)(2,1)S(1)} %shard_map.76.m_ref), channel_id=1, source_target_pairs={{0,4},{1,3},{2,6},{3,1},{4,0},{5,7},{6,2},{7,5},{8,12},{9,11},{10,... | collective-permute-start | bytes 1572872 | tf_op jit(solution)/shard_map/ppermute | solution.py:258
  18.1 0.0 collective-permute-start.3
  18.1 6.3 %shard_map.77 = (bf16[1024,1792]{1,0:T(8,128)(2,1)S(1)}, bf16[1024,1792]{1,0:T(8,128)(2,1)S(1)}, bf16[1024,1792]{1,0:T(8,128)(2,1)S(1)}, bf16[1024,1792]{1,0:T(8,128)(2,1)S(1)}, bf16[1024,1792]{1,0:T(8,128)(2,1)S(1)}) custom-call(bf16[8192,1792]{1,0:T(8,128)(2,1)} %refs_5_.7, bf16[8192,1792]{1,0:T(8,128)(2,1)} %refs_6_.7), custom_call_target="tpu_custom_call" | custom-call | bytes 1000 | tf_op jit(solution)/shard_map/pallas_call | solution.py:51
  24.5 0.8 %collective-permute-done.4.r_ref = bf16[32,8192]{1,0:T(8,128)(2,1)S(1)} collective-permute-done((bf16[32,8192]{1,0:T(8,128)(2,1)S(1)}, bf16[32,8192]{1,0:T(8,128)(2,1)S(1)}, u32[]{:S(2)}, u32[]{:S(2)}) %collective-permute-start.4) | collective-permute-done | bytes 524320 | tf_op jit(solution)/shard_map/ppermute | solution.py:258
  25.3 0.0 collective-permute-done.3.a_ref
  25.3 0.0 collective-permute-start.5
  25.3 0.1 shard_map.78.m_ref.x_ref
  25.4 0.0 copy-done
  25.4 0.4 shard_map.81.refs_0_
  25.8 3.0 %collective-permute-start.6 = (f32[64,128]{1,0:T(8,128)S(1)}, f32[64,128]{1,0:T(8,128)S(1)}, u32[]{:S(2)}, u32[]{:S(2)}) collective-permute-start(f32[64,128]{1,0:T(8,128)S(1)} %shard_map.81.refs_0_), channel_id=1, source_target_pairs={{0,8},{1,9},{2,10},{3,11},{4,12},{5,13},{6,14},{7,15},{8,0},{9,1},... | collective-permute-start | bytes 98312 | tf_op jit(solution)/shard_map/ppermute | solution.py:258
  28.9 0.0 collective-permute-done.5.r_ref
  28.9 0.1 shard_map.79.refs_0_.refs_2_.x_ref
  29.1 2.1 %shard_map.80 = (f32[128,1792]{1,0:T(8,128)S(1)}, f32[128,1792]{1,0:T(8,128)S(1)}, bf16[1024,1792]{1,0:T(8,128)(2,1)S(1)}) custom-call(bf16[128,8192]{1,0:T(8,128)(2,1)S(1)} %shard_map.79.refs_0_.refs_2_.x_ref, bf16[1024,1792]{1,0:T(8,128)(2,1)S(1)} %get-tuple-element.60.refs_1_, bf16[1024,1792]{1,0:T(8,128)(2,1)S(1)} %get-tuple-element.61.refs_2_, ...), custom_call_target="tpu_custom_call" | custom-call | bytes 1000 | tf_op jit(solution)/shard_map/pallas_call | solution.py:51
  31.2 0.0 collective-permute-done.6.refs_1_
  31.2 2.1 %collective-permute-start.7 = (f32[64,128]{1,0:T(8,128)S(1)}, f32[64,128]{1,0:T(8,128)S(1)}, u32[]{:S(2)}, u32[]{:S(2)}) collective-permute-start(f32[64,128]{1,0:T(8,128)S(1)} %shard_map.82.refs_0_), channel_id=1, source_target_pairs={{0,4},{1,5},{2,6},{3,7},{4,0},{5,1},{6,2},{7,3},{8,12},{9,13},{10,... | collective-permute-start | bytes 98312 | tf_op jit(solution)/shard_map/ppermute | solution.py:258
  33.3 3.2 %shard_map.83 = (f32[128,1792]{1,0:T(8,128)S(1)}, f32[128,1792]{1,0:T(8,128)S(1)}, bf16[1024,1792]{1,0:T(8,128)(2,1)S(1)}, bf16[1024,1792]{1,0:T(8,128)(2,1)S(1)}) custom-call(bf16[128,8192]{1,0:T(8,128)(2,1)S(1)} %shard_map.79.refs_0_.refs_2_.x_ref, bf16[1024,1792]{1,0:T(8,128)(2,1)S(1)} %get-tuple-element.69.refs_1_, ...), custom_call_target="tpu_custom_call", output_to_operand_aliasing={{0}: (7, {}), {1}: (8, {})} | custom-call | bytes 1000 | tf_op jit(solution)/shard_map/pallas_call | solution.py:51
  36.4 0.0 collective-permute-done.7.refs_1_
  36.5 1.6 %collective-permute-start.8 = (f32[64,128]{1,0:T(8,128)S(1)}, f32[64,128]{1,0:T(8,128)S(1)}, u32[]{:S(2)}, u32[]{:S(2)}) collective-permute-start(f32[64,128]{1,0:T(8,128)S(1)} %shard_map.85.refs_0_), channel_id=1, source_target_pairs={{0,2},{1,3},{2,0},{3,1},{4,6},{5,7},{6,4},{7,5},{8,10},{9,11},{10,... | collective-permute-start | bytes 98312 | tf_op jit(solution)/shard_map/ppermute | solution.py:258
  38.1 3.2 %shard_map.84 = (f32[128,1792]{1,0:T(8,128)S(1)}, f32[128,1792]{1,0:T(8,128)S(1)}, bf16[1024,1792]{1,0:T(8,128)(2,1)S(1)}, bf16[1024,1792]{1,0:T(8,128)(2,1)S(1)}) custom-call(bf16[128,8192]{1,0:T(8,128)(2,1)S(1)} %shard_map.79.refs_0_.refs_2_.x_ref, bf16[1024,1792]{1,0:T(8,128)(2,1)S(1)} %get-tuple-element.57.refs_1_, ...), custom_call_target="tpu_custom_call", output_to_operand_aliasing={{0}: (7, {}), {1}: (8, {})} | custom-call | bytes 1000 | tf_op jit(solution)/shard_map/pallas_call | solution.py:51
  41.2 0.0 collective-permute-done.8.refs_1_
  41.3 0.1 collective-permute-start.9
  41.3 2.1 %shard_map.86 = (f32[128,1792]{1,0:T(8,128)S(1)}, f32[128,1792]{1,0:T(8,128)S(1)}, bf16[512,1792]{1,0:T(8,128)(2,1)S(1)}, bf16[512,1792]{1,0:T(8,128)(2,1)S(1)}) custom-call(bf16[512,1792]{1,0:T(8,128)(2,1)} %bitcast.3, bf16[512,1792]{1,0:T(8,128)(2,1)} %bitcast.4, ...), custom_call_target="tpu_custom_call", output_to_operand_aliasing={{0}: (7, {}), {1}: (8, {})} | custom-call | bytes 1000 | tf_op jit(solution)/shard_map/pallas_call | solution.py:51
  43.4 0.0 collective-permute-done.9.refs_5_
  43.4 2.4 %shard_map.88 = bf16[128,1792]{1,0:T(8,128)(2,1)} custom-call(bf16[128,8192]{1,0:T(8,128)(2,1)S(1)} %shard_map.79.refs_0_.refs_2_.x_ref, bf16[1024,1792]{1,0:T(8,128)(2,1)S(1)} %get-tuple-element.78.refs_0_, bf16[1024,1792]{1,0:T(8,128)(2,1)S(1)} %get-tuple-element.79.refs_1_, f32[128,1792]{1,0:T(8,128)S(1)} %get-tuple-element.86.refs_2_, ...), custom_call_target="tpu_custom_call" | custom-call | tf_op jit(solution)/shard_map/pallas_call | solution.py:51
  (3 shorter events, 0.0 us)
Async XLA Ops:
  0.0 6.2 %collective-permute-start.1 = (bf16[8,512,128]{2,1,0:T(8,128)(2,1)}, bf16[8,512,128]{2,1,0:T(8,128)(2,1)S(1)}, u32[]{:S(2)}, u32[]{:S(2)}) collective-permute-start(bf16[8,512,128]{2,1,0:T(8,128)(2,1)} %d_ref.1), channel_id=1, source_target_pairs={{0,1},{1,0},{2,3},{3,2},{4,5},{5,4},{6,7},{7,6},{8,9},{9,8},{10,11... | collective-permute-start | bytes 3145736 | tf_op jit(solution)/shard_map/ppermute | solution.py:258
  0.5 5.8 %collective-permute-start = (bf16[8,8192]{1,0:T(8,128)(2,1)}, bf16[8,8192]{1,0:T(8,128)(2,1)S(1)}, u32[]{:S(2)}, u32[]{:S(2)}) collective-permute-start(bf16[8,8192]{1,0:T(8,128)(2,1)} %m_ref.1), channel_id=1, source_target_pairs={{0,2},{1,9},{2,0},{3,11},{4,6},{5,13},{6,4},{7,15},{8,10},{9,1},{1... | collective-permute-start | bytes 393224 | tf_op jit(solution)/shard_map/ppermute | solution.py:258
  3.0 3.3 %copy-start.1 = (bf16[8,8192]{1,0:T(8,128)(2,1)S(1)}, bf16[8,8192]{1,0:T(8,128)(2,1)}, u32[]{:S(2)}) copy-start(bf16[8,8192]{1,0:T(8,128)(2,1)} %m_ref.1) | copy-start | bytes 393220
  6.3 9.3 %collective-permute-start.2 = (bf16[16,8192]{1,0:T(8,128)(2,1)S(1)}, bf16[16,8192]{1,0:T(8,128)(2,1)S(1)}, u32[]{:S(2)}, u32[]{:S(2)}) collective-permute-start(bf16[16,8192]{1,0:T(8,128)(2,1)S(1)} %shard_map.74.m_ref), channel_id=1, source_target_pairs={{0,8},{1,5},{2,10},{3,7},{4,12},{5,1},{6,14},{7,3},{8,0},{9,13},{1... | collective-permute-start | bytes 786440 | tf_op jit(solution)/shard_map/ppermute | solution.py:258
  15.7 9.7 %copy-start = (bf16[8,512,128]{2,1,0:T(8,128)(2,1)S(1)}, bf16[8,512,128]{2,1,0:T(8,128)(2,1)}, u32[]{:S(2)}) copy-start(bf16[8,512,128]{2,1,0:T(8,128)(2,1)} %d_ref.1) | copy-start | bytes 3145732
  15.7 9.5 %collective-permute-start.4 = (bf16[32,8192]{1,0:T(8,128)(2,1)S(1)}, bf16[32,8192]{1,0:T(8,128)(2,1)S(1)}, u32[]{:S(2)}, u32[]{:S(2)}) collective-permute-start(bf16[32,8192]{1,0:T(8,128)(2,1)S(1)} %shard_map.76.m_ref), channel_id=1, source_target_pairs={{0,4},{1,3},{2,6},{3,1},{4,0},{5,7},{6,2},{7,5},{8,12},{9,11},{10,... | collective-permute-start | bytes 1572872 | tf_op jit(solution)/shard_map/ppermute | solution.py:258
  18.1 7.2 %collective-permute-start.3 = (bf16[32,8192]{1,0:T(8,128)(2,1)S(1)}, bf16[32,8192]{1,0:T(8,128)(2,1)S(1)}, u32[]{:S(2)}, u32[]{:S(2)}) collective-permute-start(bf16[32,8192]{1,0:T(8,128)(2,1)S(1)} %shard_map.76.m_ref), channel_id=1, source_target_pairs={{0,1},{1,0},{2,3},{3,2},{4,5},{5,4},{6,7},{7,6},{8,9},{9,8},{10,11... | collective-permute-start | bytes 1572872 | tf_op jit(solution)/shard_map/ppermute | solution.py:258
  25.3 3.6 %collective-permute-start.5 = (bf16[32,8192]{1,0:T(8,128)(2,1)S(1)}, bf16[32,8192]{1,0:T(8,128)(2,1)S(1)}, u32[]{:S(2)}, u32[]{:S(2)}) collective-permute-start(bf16[32,8192]{1,0:T(8,128)(2,1)S(1)} %collective-permute-done.4.r_ref), channel_id=1, source_target_pairs={{0,1},{1,0},{2,3},{3,2},{4,5},{5,4},{6,7},{7,6},{8,9},{9,8},{10,11... | collective-permute-start | bytes 1572872 | tf_op jit(solution)/shard_map/ppermute | solution.py:258
  25.8 5.3 %collective-permute-start.6 = (f32[64,128]{1,0:T(8,128)S(1)}, f32[64,128]{1,0:T(8,128)S(1)}, u32[]{:S(2)}, u32[]{:S(2)}) collective-permute-start(f32[64,128]{1,0:T(8,128)S(1)} %shard_map.81.refs_0_), channel_id=1, source_target_pairs={{0,8},{1,9},{2,10},{3,11},{4,12},{5,13},{6,14},{7,15},{8,0},{9,1},... | collective-permute-start | bytes 98312 | tf_op jit(solution)/shard_map/ppermute | solution.py:258
  31.2 5.3 %collective-permute-start.7 = (f32[64,128]{1,0:T(8,128)S(1)}, f32[64,128]{1,0:T(8,128)S(1)}, u32[]{:S(2)}, u32[]{:S(2)}) collective-permute-start(f32[64,128]{1,0:T(8,128)S(1)} %shard_map.82.refs_0_), channel_id=1, source_target_pairs={{0,4},{1,5},{2,6},{3,7},{4,0},{5,1},{6,2},{7,3},{8,12},{9,13},{10,... | collective-permute-start | bytes 98312 | tf_op jit(solution)/shard_map/ppermute | solution.py:258
  36.5 4.8 %collective-permute-start.8 = (f32[64,128]{1,0:T(8,128)S(1)}, f32[64,128]{1,0:T(8,128)S(1)}, u32[]{:S(2)}, u32[]{:S(2)}) collective-permute-start(f32[64,128]{1,0:T(8,128)S(1)} %shard_map.85.refs_0_), channel_id=1, source_target_pairs={{0,2},{1,3},{2,0},{3,1},{4,6},{5,7},{6,4},{7,5},{8,10},{9,11},{10,... | collective-permute-start | bytes 98312 | tf_op jit(solution)/shard_map/ppermute | solution.py:258
  41.3 2.2 %collective-permute-start.9 = (f32[64,128]{1,0:T(8,128)S(1)}, f32[64,128]{1,0:T(8,128)S(1)}, u32[]{:S(2)}, u32[]{:S(2)}) collective-permute-start(f32[64,128]{1,0:T(8,128)S(1)} %shard_map.87.refs_4_), channel_id=1, source_target_pairs={{0,1},{1,0},{2,3},{3,2},{4,5},{5,4},{6,7},{7,6},{8,9},{9,8},{10,11... | collective-permute-start | bytes 98312 | tf_op jit(solution)/shard_map/ppermute | solution.py:258
